TPU v7x, 32 devices: a whole 2x2x4 slice. The times are simulated.
32 devices in a mesh: grp: 2 (over x), rank: 16 (over z, y, core).
Axes of the slice: x: 2, y: 2, z: 4, core: 2. Of those that a mesh axis runs over, the one named last changes fastest.
Arguments:
- multipole: bfloat16 [888, 8192], P(None, ('grp', 'rank')), may hold values from -6 to 6
- compress: bfloat16 [256, 888], replicated, may hold values from -0.1875 to 0.1875
- expand: bfloat16 [888, 256], replicated, may hold values from -0.375 to 0.375
- octant_ops: bfloat16 [8, 256, 256], replicated, may hold values from -0.125 to 0.125
- far_ops: bfloat16 [16, 256, 256], replicated, may hold values from -0.1875 to 0.1875
- list_seven: int32 [16, 8192], P(None, ('grp', 'rank')), may hold values from -1 to 8191, as said below
- list_six: int32 [16, 1024], P(None, ('grp', 'rank')), may hold values from -1 to 1023, as said below
- list_five: int32 [16, 128], P(None, ('grp', 'rank')), may hold values from -1 to 127, as said below
- list_four: int32 [16, 16], replicated, may hold values from -1 to 15, as said below
- list_three: int32 [16, 2], replicated, may hold values from -1 to 1, as said below
Outputs:
- potential_coef: float32 [888, 8192], P(None, ('grp', 'rank'))
Inputs may be any that keep to these rules, and one draw needn't show every extreme that they name: `list_seven`: entry [c, t] is the source box of box t of the finest level for class c, or -1; a source differs from its target by at most 256. `list_six`: as list_seven for the second finest level; a source differs from its target by at most 32. `list_five`: as list_seven for the third finest level; a source differs from its target by at most 4. `list_four`: entry [c, t] is the source box of box t for class c, or -1. `list_three`: entry [c, t] is the source box of box t for class c, or -1.
All inputs are finite; a program needn't handle non-finite values.
Results may differ from a plain program's by a relative error of at most 0.0085.
Values may be sent and summed in bfloat16 or wider, within the bound.
A program may use at most 64 MiB of HBM per device.

v0:
```python
import jax
import jax.numpy as jnp
from jax import lax
from jax.sharding import PartitionSpec as P


def extended(cells, sides, width):
    for axis, dim in sides:
        count = lax.axis_size(axis)
        ends = count - 1
        head = lax.slice_in_dim(cells, 0, width, axis=dim)
        tail = lax.slice_in_dim(cells, cells.shape[dim] - width, cells.shape[dim], axis=dim)
        cells = jnp.concatenate(
            [
                lax.ppermute(tail, axis, [(i, (i + 1) % count) for i in range(ends)]),
                cells,
                lax.ppermute(head, axis, [((i + 1) % count, i) for i in range(ends)]),
            ],
            axis=dim,
        )
    return cells


def ascend(coef, octant_ops):
    rows, count = coef.shape
    grouped = coef.reshape(rows, count // 8, 8)
    parent = jnp.einsum("oij,jpo->ip", octant_ops, grouped, preferred_element_type=jnp.float32)
    return parent.astype(jnp.bfloat16)


def descend(local, octant_ops):
    rows, count = local.shape
    rounded = local.astype(jnp.bfloat16)
    spread = jnp.einsum("oji,jp->ipo", octant_ops, rounded, preferred_element_type=jnp.float32)
    return spread.reshape(rows, count * 8)


def interact(coef, entries, far_ops, anchor):
    summed = jnp.zeros((coef.shape[0], entries.shape[1]), jnp.float32)
    for member in range(entries.shape[0]):
        present = entries[member] >= 0
        located = jnp.where(present, entries[member] - anchor, 0)
        picked = jnp.take(coef, located, axis=1)
        picked = jnp.where(present[None, :], picked, jnp.zeros_like(picked))
        summed = summed + jnp.dot(far_ops[member], picked, preferred_element_type=jnp.float32)
    return summed


def on_device(
    multipole,
    compress,
    expand,
    octant_ops,
    far_ops,
    list_seven,
    list_six,
    list_five,
    list_four,
    list_three,
):
    coef_seven = jnp.dot(compress, multipole, preferred_element_type=jnp.float32).astype(
        jnp.bfloat16
    )
    coef_six = ascend(coef_seven, octant_ops)
    coef_five = ascend(coef_six, octant_ops)
    count_seven = coef_seven.shape[1]
    count_six = coef_six.shape[1]
    count_five = coef_five.shape[1]
    breadth = count_seven + count_six + count_five
    stacked = jnp.concatenate([coef_seven, coef_six, coef_five], axis=1)
    padded = extended(stacked, ((("grp", "rank"), 1),), breadth)
    before = padded[:, :breadth]
    after = padded[:, 2 * breadth :]
    device = lax.axis_index(("grp", "rank"))

    def beside_all(coef, offset, count):
        return jnp.concatenate(
            [before[:, offset : offset + count], coef, after[:, offset : offset + count]], axis=1
        )

    far_seven = interact(
        beside_all(coef_seven, 0, count_seven),
        list_seven,
        far_ops,
        device * count_seven - count_seven,
    )
    far_six = (
        interact(
            beside_all(coef_six, count_seven, count_six),
            list_six,
            far_ops,
            device * count_six - count_six,
        )
        * 2.0
    )
    far_five = (
        interact(
            beside_all(coef_five, count_seven + count_six, count_five),
            list_five,
            far_ops,
            device * count_five - count_five,
        )
        * 4.0
    )
    gathered = lax.all_gather(coef_five, ("grp", "rank"), axis=1, tiled=True)
    coef_four = ascend(gathered, octant_ops)
    coef_three = ascend(coef_four, octant_ops)
    owned_four = max(1, count_five // 8)
    owned_three = max(1, count_five // 64)
    start_four = device * count_five // 8
    start_three = device * count_five // 64
    entries_four = lax.dynamic_slice_in_dim(list_four, start_four, owned_four, 1)
    entries_three = lax.dynamic_slice_in_dim(list_three, start_three, owned_three, 1)
    far_four = interact(coef_four, entries_four, far_ops, 0) * 8.0
    far_three = interact(coef_three, entries_three, far_ops, 0) * 16.0
    spread_three = descend(far_three, octant_ops)
    local_four = far_four + lax.dynamic_slice_in_dim(
        spread_three, start_four - start_three * 8, owned_four, 1
    )
    parents = descend(local_four, octant_ops)
    local_five = far_five + lax.dynamic_slice_in_dim(
        parents, device * count_five - start_four * 8, count_five, 1
    )
    local_six = far_six + descend(local_five, octant_ops)
    local_seven = far_seven + descend(local_six, octant_ops)
    return jnp.dot(expand, local_seven.astype(jnp.bfloat16), preferred_element_type=jnp.float32)


def solution(mesh):
    return jax.shard_map(
        on_device,
        mesh=mesh,
        in_specs=(
            P(None, ("grp", "rank")),
            P(),
            P(),
            P(),
            P(),
            P(None, ("grp", "rank")),
            P(None, ("grp", "rank")),
            P(None, ("grp", "rank")),
            P(),
            P(),
        ),
        out_specs=P(None, ("grp", "rank")),
        check_vma=False,
    )
```

profile of v0, /device:TPU:0, one launch (start us, length us, event | category | flops | bytes accessed | tf_op | source)
XLA Modules:
  0.0 233.2 jit_solution(12626409982333168097)
XLA Ops:
  0.0 1.6 convolution_convert_fusion
  2.5 3.2 %collective-permute-start = (bf16[256,292]{0,1:T(8,128)(2,1)S(1)}, bf16[256,292]{0,1:T(8,128)(2,1)}, u32[]{:S(2)}, u32[]{:S(2)}) collective-permute-start(bf16[256,292]{0,1:T(8,128)(2,1)S(1)} %pad_maximum_fusion.1), channel_id=1, source_target_pairs={{0,1},{1,2},{2,3},{3,4},{4,5},{5,6},{6,7},{7,8},{8,9},{9,10},{10,1... | collective-permute-start | bytes 448520 | tf_op jit(solution)/shard_map/ppermute | solution.py:15
  5.6 1.3 collective-permute-start.1
  48.6 1.0 fusion.736
  62.4 44.8 %all-gather = bf16[32,4,256]{2,1,0:T(4,128)(2,1)S(1)} all-gather(bf16[1,4,256]{2,1,0:T(4,128)(2,1)S(1)} %bitcast.750), channel_id=1, replica_groups=mesh['grp'=2,'rank'=16] {'grp','rank'}, dimensions={0}, use_global_device_ids=true | all-gather | bytes 67584 | tf_op jit(solution)/shard_map/all_gather | solution.py:105
  128.5 1.2 gather_fusion.32
  129.6 1.1 gather_fusion.33
  130.8 1.1 gather_fusion.34
  131.9 1.1 gather_fusion.35
  133.1 1.1 gather_fusion.36
  134.2 1.1 gather_fusion.37
  135.3 1.2 gather_fusion.38
  136.4 1.1 gather_fusion.39
  137.6 1.1 gather_fusion.40
  138.7 1.1 gather_fusion.41
  139.8 1.2 gather_fusion.42
  141.0 1.1 gather_fusion.43
  145.8 1.2 gather_fusion.16
  147.1 1.2 gather_fusion.17
  148.3 1.2 gather_fusion.18
  149.5 1.2 gather_fusion.19
  150.7 1.2 gather_fusion.20
  152.0 1.2 gather_fusion.21
  153.2 1.2 gather_fusion.22
  154.4 1.2 gather_fusion.23
  155.6 1.2 gather_fusion.24
  156.9 1.2 gather_fusion.25
  158.1 1.2 gather_fusion.26
  159.3 1.2 gather_fusion.27
  160.5 1.2 gather_fusion.28
  161.8 1.2 gather_fusion.29
  163.0 1.2 gather_fusion.30
  164.2 1.2 gather_fusion.31
  165.4 0.9 slice.662
  166.3 0.9 slice.663
  167.3 0.9 pad_maximum_fusion
  168.2 1.9 gather_fusion
  170.1 1.9 gather_fusion.1
  172.1 1.9 gather_fusion.2
  174.0 1.9 gather_fusion.3
  176.0 1.9 gather_fusion.4
  177.9 1.9 gather_fusion.5
  179.8 1.9 gather_fusion.6
  181.8 1.9 gather_fusion.7
  183.7 1.9 gather_fusion.8
  185.6 1.9 gather_fusion.9
  187.6 1.9 gather_fusion.10
  189.5 2.2 gather_fusion.11
  191.7 1.9 gather_fusion.12
  193.6 1.9 gather_fusion.13
  195.6 1.9 gather_fusion.14
  197.5 1.9 gather_fusion.15
  200.4 1.0 fusion.134
  201.4 1.2 fusion.136
  203.4 0.9 convolution_add_fusion.43
  204.3 0.9 convolution_add_fusion.42
  205.2 0.9 convolution_add_fusion.41
  207.0 0.9 convolution_add_fusion.39
  207.8 0.9 convolution_add_fusion.38
  213.4 0.9 convolution_add_fusion.27
  216.0 0.9 convolution_add_fusion.24
  226.9 1.7 convolution_bitcast_fusion.2
  228.6 2.0 convolution_bitcast_fusion.1
  230.6 2.6 %convolution_bitcast_fusion = f32[888,256]{1,0:T(8,128)} fusion(bf16[888,256]{1,0:T(8,128)(2,1)} %param.22, f32[256,256]{1,0:T(8,128)S(1)} %convolution_add_fusion.1, f32[256,32,8]{0,1,2:T(8,128)} %convolution_bitcast_fusion.1, bf16[256,256]{1,0:T(8,128)(2,1)S(1)} %copy-done.21, pred[256]{0:T(512)(128)(4,1)} %get-tuple-element.300, ...), kind=kOutput, calls=%fused_computation.48 | convolution fusion | flops 150274048 | bytes 2150912 | tf_op jit(solution)/shard_map/dot_general | solution.py:126
  (380 shorter events, 57.6 us)
Async XLA Ops:
  0.0 6.9 %copy-start.101 = (s32[16,2]{0,1:T(2,128)S(1)}, s32[16,2]{0,1:T(2,128)}, u32[]{:S(2)}) copy-start(s32[16,2]{0,1:T(2,128)} %param.29) | copy-start | bytes 388
  0.0 27.7 %copy-start.39 = (s32[16,16]{1,0:T(8,128)S(1)}, s32[16,16]{1,0:T(8,128)}, u32[]{:S(2)}) copy-start(s32[16,16]{1,0:T(8,128)} %param.28) | copy-start | bytes 3076
  0.0 48.6 %copy-start.2 = (s32[16,4]{0,1:T(4,128)S(1)}, s32[16,4]{0,1:T(4,128)}, u32[]{:S(2)}) copy-start(s32[16,4]{0,1:T(4,128)} %param.27) | copy-start | bytes 772
  0.0 57.7 %copy-start.36 = (s32[16,256]{1,0:T(8,128)S(1)}, s32[16,256]{1,0:T(8,128)}, u32[]{:S(2)}) copy-start(s32[16,256]{1,0:T(8,128)} %param.25) | copy-start | bytes 49156
  2.4 105.6 %copy-start.1 = (bf16[16,256,256]{2,1,0:T(8,128)(2,1)S(1)}, bf16[16,256,256]{2,1,0:T(8,128)(2,1)}, u32[]{:S(2)}) copy-start(bf16[16,256,256]{2,1,0:T(8,128)(2,1)} %param.24) | copy-start | bytes 6291460
  2.5 124.6 %collective-permute-start = (bf16[256,292]{0,1:T(8,128)(2,1)S(1)}, bf16[256,292]{0,1:T(8,128)(2,1)}, u32[]{:S(2)}, u32[]{:S(2)}) collective-permute-start(bf16[256,292]{0,1:T(8,128)(2,1)S(1)} %pad_maximum_fusion.1), channel_id=1, source_target_pairs={{0,1},{1,2},{2,3},{3,4},{4,5},{5,6},{6,7},{7,8},{8,9},{9,10},{10,1... | collective-permute-start | bytes 448520 | tf_op jit(solution)/shard_map/ppermute | solution.py:15
  5.6 122.2 %collective-permute-start.1 = (bf16[256,292]{0,1:T(8,128)(2,1)S(1)}, bf16[256,292]{0,1:T(8,128)(2,1)}, u32[]{:S(2)}, u32[]{:S(2)}) collective-permute-start(bf16[256,292]{0,1:T(8,128)(2,1)S(1)} %pad_maximum_fusion.1), channel_id=1, source_target_pairs={{1,0},{2,1},{3,2},{4,3},{5,4},{6,5},{7,6},{8,7},{9,8},{10,9},{11,1... | collective-permute-start | bytes 448520 | tf_op jit(solution)/shard_map/ppermute | solution.py:17
  111.1 3.8 %copy-start.37 = (s32[16,32]{1,0:T(8,128)S(1)}, s32[16,32]{1,0:T(8,128)}, u32[]{:S(2)}) copy-start(s32[16,32]{1,0:T(8,128)} %param.26) | copy-start | bytes 6148
  199.4 10.2 %copy-start.6 = (bf16[4,256]{1,0:T(4,128)(2,1)S(1)}, bf16[4,256]{1,0:T(4,128)(2,1)}, u32[]{:S(2)}) copy-start(bf16[4,256]{1,0:T(4,128)(2,1)} %gather_fusion.41) | copy-start | bytes 6148
  199.4 10.2 %copy-start.83 = (pred[4]{0:T(512)(128)(4,1)S(1)}, pred[4]{0:T(512)(128)(4,1)}, u32[]{:S(2)}) copy-start(pred[4]{0:T(512)(128)(4,1)} %get-tuple-element.212) | copy-start | bytes 16
  199.4 10.2 %copy-start.99 = (pred[4]{0:T(512)(128)(4,1)S(1)}, pred[4]{0:T(512)(128)(4,1)}, u32[]{:S(2)}) copy-start(pred[4]{0:T(512)(128)(4,1)} %get-tuple-element.290) | copy-start | bytes 16
  199.4 10.5 %copy-start.5 = (bf16[4,256]{1,0:T(4,128)(2,1)S(1)}, bf16[4,256]{1,0:T(4,128)(2,1)}, u32[]{:S(2)}) copy-start(bf16[4,256]{1,0:T(4,128)(2,1)} %gather_fusion.42) | copy-start | bytes 6148
  199.4 10.5 %copy-start.82 = (pred[4]{0:T(512)(128)(4,1)S(1)}, pred[4]{0:T(512)(128)(4,1)}, u32[]{:S(2)}) copy-start(pred[4]{0:T(512)(128)(4,1)} %get-tuple-element.210) | copy-start | bytes 16
  199.4 10.5 %copy-start.100 = (pred[4]{0:T(512)(128)(4,1)S(1)}, pred[4]{0:T(512)(128)(4,1)}, u32[]{:S(2)}) copy-start(pred[4]{0:T(512)(128)(4,1)} %get-tuple-element.289) | copy-start | bytes 16
  199.4 10.6 %copy-start.4 = (bf16[4,256]{1,0:T(4,128)(2,1)S(1)}, bf16[4,256]{1,0:T(4,128)(2,1)}, u32[]{:S(2)}) copy-start(bf16[4,256]{1,0:T(4,128)(2,1)} %gather_fusion.43) | copy-start | bytes 6148
  199.5 10.6 %copy-start.81 = (pred[4]{0:T(512)(128)(4,1)S(1)}, pred[4]{0:T(512)(128)(4,1)}, u32[]{:S(2)}) copy-start(pred[4]{0:T(512)(128)(4,1)} %get-tuple-element.208) | copy-start | bytes 16
  199.5 10.6 %copy-start.97 = (pred[4]{0:T(512)(128)(4,1)S(1)}, pred[4]{0:T(512)(128)(4,1)}, u32[]{:S(2)}) copy-start(pred[4]{0:T(512)(128)(4,1)} %get-tuple-element.288) | copy-start | bytes 16
  199.5 10.8 %copy-start.80 = (pred[4]{0:T(512)(128)(4,1)S(1)}, pred[4]{0:T(512)(128)(4,1)}, u32[]{:S(2)}) copy-start(pred[4]{0:T(512)(128)(4,1)} %get-tuple-element.206) | copy-start | bytes 16
  199.5 10.8 %copy-start.98 = (pred[4]{0:T(512)(128)(4,1)S(1)}, pred[4]{0:T(512)(128)(4,1)}, u32[]{:S(2)}) copy-start(pred[4]{0:T(512)(128)(4,1)} %get-tuple-element.287) | copy-start | bytes 16
  199.5 11.0 %copy-start.79 = (pred[4]{0:T(512)(128)(4,1)S(1)}, pred[4]{0:T(512)(128)(4,1)}, u32[]{:S(2)}) copy-start(pred[4]{0:T(512)(128)(4,1)} %get-tuple-element.70) | copy-start | bytes 16
  199.5 11.0 %copy-start.96 = (pred[4]{0:T(512)(128)(4,1)S(1)}, pred[4]{0:T(512)(128)(4,1)}, u32[]{:S(2)}) copy-start(pred[4]{0:T(512)(128)(4,1)} %get-tuple-element.286) | copy-start | bytes 16
  199.5 11.2 %copy-start.78 = (pred[4]{0:T(512)(128)(4,1)S(1)}, pred[4]{0:T(512)(128)(4,1)}, u32[]{:S(2)}) copy-start(pred[4]{0:T(512)(128)(4,1)} %get-tuple-element.234) | copy-start | bytes 16
  199.5 12.1 %copy-start.35 = (bf16[32,256]{1,0:T(8,128)(2,1)S(1)}, bf16[32,256]{1,0:T(8,128)(2,1)}, u32[]{:S(2)}) copy-start(bf16[32,256]{1,0:T(8,128)(2,1)} %gather_fusion.17) | copy-start | bytes 49156
  199.5 12.1 %copy-start.95 = (pred[32]{0:T(512)(128)(4,1)S(1)}, pred[32]{0:T(512)(128)(4,1)}, u32[]{:S(2)}) copy-start(pred[32]{0:T(512)(128)(4,1)} %get-tuple-element.157) | copy-start | bytes 100
  199.5 12.9 %copy-start.34 = (bf16[32,256]{1,0:T(8,128)(2,1)S(1)}, bf16[32,256]{1,0:T(8,128)(2,1)}, u32[]{:S(2)}) copy-start(bf16[32,256]{1,0:T(8,128)(2,1)} %gather_fusion.18) | copy-start | bytes 49156
  199.6 13.8 %copy-start.33 = (bf16[32,256]{1,0:T(8,128)(2,1)S(1)}, bf16[32,256]{1,0:T(8,128)(2,1)}, u32[]{:S(2)}) copy-start(bf16[32,256]{1,0:T(8,128)(2,1)} %gather_fusion.19) | copy-start | bytes 49156
  200.4 13.9 %copy-start.32 = (bf16[32,256]{1,0:T(8,128)(2,1)S(1)}, bf16[32,256]{1,0:T(8,128)(2,1)}, u32[]{:S(2)}) copy-start(bf16[32,256]{1,0:T(8,128)(2,1)} %gather_fusion.20) | copy-start | bytes 49156
  201.4 13.7 %copy-start.31 = (bf16[32,256]{1,0:T(8,128)(2,1)S(1)}, bf16[32,256]{1,0:T(8,128)(2,1)}, u32[]{:S(2)}) copy-start(bf16[32,256]{1,0:T(8,128)(2,1)} %gather_fusion.21) | copy-start | bytes 49156
  201.4 14.6 %copy-start.30 = (bf16[32,256]{1,0:T(8,128)(2,1)S(1)}, bf16[32,256]{1,0:T(8,128)(2,1)}, u32[]{:S(2)}) copy-start(bf16[32,256]{1,0:T(8,128)(2,1)} %gather_fusion.22) | copy-start | bytes 49156
  202.6 14.3 %copy-start.29 = (bf16[32,256]{1,0:T(8,128)(2,1)S(1)}, bf16[32,256]{1,0:T(8,128)(2,1)}, u32[]{:S(2)}) copy-start(bf16[32,256]{1,0:T(8,128)(2,1)} %gather_fusion.23) | copy-start | bytes 49156
  203.4 14.3 %copy-start.28 = (bf16[32,256]{1,0:T(8,128)(2,1)S(1)}, bf16[32,256]{1,0:T(8,128)(2,1)}, u32[]{:S(2)}) copy-start(bf16[32,256]{1,0:T(8,128)(2,1)} %gather_fusion.24) | copy-start | bytes 49156
  204.3 14.2 %copy-start.27 = (bf16[32,256]{1,0:T(8,128)(2,1)S(1)}, bf16[32,256]{1,0:T(8,128)(2,1)}, u32[]{:S(2)}) copy-start(bf16[32,256]{1,0:T(8,128)(2,1)} %gather_fusion.25) | copy-start | bytes 49156
  205.2 14.2 %copy-start.26 = (bf16[32,256]{1,0:T(8,128)(2,1)S(1)}, bf16[32,256]{1,0:T(8,128)(2,1)}, u32[]{:S(2)}) copy-start(bf16[32,256]{1,0:T(8,128)(2,1)} %gather_fusion.26) | copy-start | bytes 49156
  206.1 14.3 %copy-start.25 = (bf16[32,256]{1,0:T(8,128)(2,1)S(1)}, bf16[32,256]{1,0:T(8,128)(2,1)}, u32[]{:S(2)}) copy-start(bf16[32,256]{1,0:T(8,128)(2,1)} %gather_fusion.27) | copy-start | bytes 49156
  207.0 14.2 %copy-start.24 = (bf16[32,256]{1,0:T(8,128)(2,1)S(1)}, bf16[32,256]{1,0:T(8,128)(2,1)}, u32[]{:S(2)}) copy-start(bf16[32,256]{1,0:T(8,128)(2,1)} %gather_fusion.28) | copy-start | bytes 49156
  207.8 13.5 %copy-start.23 = (bf16[32,256]{1,0:T(8,128)(2,1)S(1)}, bf16[32,256]{1,0:T(8,128)(2,1)}, u32[]{:S(2)}) copy-start(bf16[32,256]{1,0:T(8,128)(2,1)} %gather_fusion.29) | copy-start | bytes 49156
  207.8 13.5 %copy-start.85 = (pred[32]{0:T(512)(128)(4,1)S(1)}, pred[32]{0:T(512)(128)(4,1)}, u32[]{:S(2)}) copy-start(pred[32]{0:T(512)(128)(4,1)} %get-tuple-element.145) | copy-start | bytes 100
  208.7 12.9 %copy-start.22 = (bf16[32,256]{1,0:T(8,128)(2,1)S(1)}, bf16[32,256]{1,0:T(8,128)(2,1)}, u32[]{:S(2)}) copy-start(bf16[32,256]{1,0:T(8,128)(2,1)} %gather_fusion.30) | copy-start | bytes 49156
  209.6 12.8 %copy-start.20 = (bf16[256,256]{1,0:T(8,128)(2,1)S(1)}, bf16[256,256]{1,0:T(8,128)(2,1)}, u32[]{:S(2)}) copy-start(bf16[256,256]{1,0:T(8,128)(2,1)} %gather_fusion.1) | copy-start | bytes 393220
  209.6 12.8 %copy-start.53 = (pred[256]{0:T(512)(128)(4,1)S(1)}, pred[256]{0:T(512)(128)(4,1)}, u32[]{:S(2)}) copy-start(pred[256]{0:T(512)(128)(4,1)} %get-tuple-element.45) | copy-start | bytes 772
  209.7 12.8 %copy-start.66 = (pred[256]{0:T(512)(128)(4,1)S(1)}, pred[256]{0:T(512)(128)(4,1)}, u32[]{:S(2)}) copy-start(pred[256]{0:T(512)(128)(4,1)} %get-tuple-element.314) | copy-start | bytes 772
  209.8 7.9 %copy-start.90 = (pred[32]{0:T(512)(128)(4,1)S(1)}, pred[32]{0:T(512)(128)(4,1)}, u32[]{:S(2)}) copy-start(pred[32]{0:T(512)(128)(4,1)} %get-tuple-element.150) | copy-start | bytes 100
  209.8 8.7 %copy-start.89 = (pred[32]{0:T(512)(128)(4,1)S(1)}, pred[32]{0:T(512)(128)(4,1)}, u32[]{:S(2)}) copy-start(pred[32]{0:T(512)(128)(4,1)} %get-tuple-element.149) | copy-start | bytes 100
  209.8 10.5 %copy-start.87 = (pred[32]{0:T(512)(128)(4,1)S(1)}, pred[32]{0:T(512)(128)(4,1)}, u32[]{:S(2)}) copy-start(pred[32]{0:T(512)(128)(4,1)} %get-tuple-element.147) | copy-start | bytes 100
  209.8 11.3 %copy-start.86 = (pred[32]{0:T(512)(128)(4,1)S(1)}, pred[32]{0:T(512)(128)(4,1)}, u32[]{:S(2)}) copy-start(pred[32]{0:T(512)(128)(4,1)} %get-tuple-element.146) | copy-start | bytes 100
  209.9 11.8 %copy-start.84 = (pred[32]{0:T(512)(128)(4,1)S(1)}, pred[32]{0:T(512)(128)(4,1)}, u32[]{:S(2)}) copy-start(pred[32]{0:T(512)(128)(4,1)} %get-tuple-element.159) | copy-start | bytes 100
  210.1 6.8 %copy-start.91 = (pred[32]{0:T(512)(128)(4,1)S(1)}, pred[32]{0:T(512)(128)(4,1)}, u32[]{:S(2)}) copy-start(pred[32]{0:T(512)(128)(4,1)} %get-tuple-element.151) | copy-start | bytes 100
  210.1 9.4 %copy-start.88 = (pred[32]{0:T(512)(128)(4,1)S(1)}, pred[32]{0:T(512)(128)(4,1)}, u32[]{:S(2)}) copy-start(pred[32]{0:T(512)(128)(4,1)} %get-tuple-element.148) | copy-start | bytes 100
  210.5 12.3 %copy-start.19 = (bf16[256,256]{1,0:T(8,128)(2,1)S(1)}, bf16[256,256]{1,0:T(8,128)(2,1)}, u32[]{:S(2)}) copy-start(bf16[256,256]{1,0:T(8,128)(2,1)} %gather_fusion.2) | copy-start | bytes 393220
  210.5 12.3 %copy-start.52 = (pred[256]{0:T(512)(128)(4,1)S(1)}, pred[256]{0:T(512)(128)(4,1)}, u32[]{:S(2)}) copy-start(pred[256]{0:T(512)(128)(4,1)} %get-tuple-element.44) | copy-start | bytes 772
  210.5 12.3 %copy-start.67 = (pred[256]{0:T(512)(128)(4,1)S(1)}, pred[256]{0:T(512)(128)(4,1)}, u32[]{:S(2)}) copy-start(pred[256]{0:T(512)(128)(4,1)} %get-tuple-element.313) | copy-start | bytes 772
  210.7 10.7 %copy-start.93 = (pred[32]{0:T(512)(128)(4,1)S(1)}, pred[32]{0:T(512)(128)(4,1)}, u32[]{:S(2)}) copy-start(pred[32]{0:T(512)(128)(4,1)} %get-tuple-element.184) | copy-start | bytes 100
  211.6 9.6 %copy-start.94 = (pred[32]{0:T(512)(128)(4,1)S(1)}, pred[32]{0:T(512)(128)(4,1)}, u32[]{:S(2)}) copy-start(pred[32]{0:T(512)(128)(4,1)} %get-tuple-element.182) | copy-start | bytes 100
  212.5 9.2 %copy-start.92 = (pred[32]{0:T(512)(128)(4,1)S(1)}, pred[32]{0:T(512)(128)(4,1)}, u32[]{:S(2)}) copy-start(pred[32]{0:T(512)(128)(4,1)} %get-tuple-element.186) | copy-start | bytes 100
  213.3 9.8 %copy-start.18 = (bf16[256,256]{1,0:T(8,128)(2,1)S(1)}, bf16[256,256]{1,0:T(8,128)(2,1)}, u32[]{:S(2)}) copy-start(bf16[256,256]{1,0:T(8,128)(2,1)} %gather_fusion.3) | copy-start | bytes 393220
  213.3 9.8 %copy-start.51 = (pred[256]{0:T(512)(128)(4,1)S(1)}, pred[256]{0:T(512)(128)(4,1)}, u32[]{:S(2)}) copy-start(pred[256]{0:T(512)(128)(4,1)} %get-tuple-element.43) | copy-start | bytes 772
  213.4 9.8 %copy-start.64 = (pred[256]{0:T(512)(128)(4,1)S(1)}, pred[256]{0:T(512)(128)(4,1)}, u32[]{:S(2)}) copy-start(pred[256]{0:T(512)(128)(4,1)} %get-tuple-element.312) | copy-start | bytes 772
  216.9 6.6 %copy-start.17 = (bf16[256,256]{1,0:T(8,128)(2,1)S(1)}, bf16[256,256]{1,0:T(8,128)(2,1)}, u32[]{:S(2)}) copy-start(bf16[256,256]{1,0:T(8,128)(2,1)} %gather_fusion.4) | copy-start | bytes 393220
  216.9 6.6 %copy-start.50 = (pred[256]{0:T(512)(128)(4,1)S(1)}, pred[256]{0:T(512)(128)(4,1)}, u32[]{:S(2)}) copy-start(pred[256]{0:T(512)(128)(4,1)} %get-tuple-element.42) | copy-start | bytes 772
  216.9 6.6 %copy-start.65 = (pred[256]{0:T(512)(128)(4,1)S(1)}, pred[256]{0:T(512)(128)(4,1)}, u32[]{:S(2)}) copy-start(pred[256]{0:T(512)(128)(4,1)} %get-tuple-element.311) | copy-start | bytes 772
  219.5 4.3 %copy-start.16 = (bf16[256,256]{1,0:T(8,128)(2,1)S(1)}, bf16[256,256]{1,0:T(8,128)(2,1)}, u32[]{:S(2)}) copy-start(bf16[256,256]{1,0:T(8,128)(2,1)} %gather_fusion.5) | copy-start | bytes 393220
  219.5 4.3 %copy-start.49 = (pred[256]{0:T(512)(128)(4,1)S(1)}, pred[256]{0:T(512)(128)(4,1)}, u32[]{:S(2)}) copy-start(pred[256]{0:T(512)(128)(4,1)} %get-tuple-element.41) | copy-start | bytes 772
  219.5 4.3 %copy-start.62 = (pred[256]{0:T(512)(128)(4,1)S(1)}, pred[256]{0:T(512)(128)(4,1)}, u32[]{:S(2)}) copy-start(pred[256]{0:T(512)(128)(4,1)} %get-tuple-element.310) | copy-start | bytes 772
  226.3 4.3 %copy-start.21 = (bf16[256,256]{1,0:T(8,128)(2,1)S(1)}, bf16[256,256]{1,0:T(8,128)(2,1)}, u32[]{:S(2)}) copy-start(bf16[256,256]{1,0:T(8,128)(2,1)} %gather_fusion.15) | copy-start | bytes 393220
  (40 other events, 87.9 us)
where the time goes:
time: 235 us; the launch traced here: 233 us
  local copies, waits for them, and re-layouts  74 us (31%)
  blocking collectives  44.8 us (19%)
  between operations  41.9 us (18%)
  matrix products  41.6 us (18%)
  other arithmetic  26.4 us (11%)
  starting transfers between devices  4.44 us (2%)
    gather x48, local copies, waits for them, and re-layouts, interact(): picked = jnp.take(coef, located, axis=1)  66.7 us
    all_gather x1, blocking collectives, on_device(): gathered = lax.all_gather(coef_five, ('grp', 'rank'), axis=1, tiled=True)  44.8 us
    dot_general x77, matrix products, interact(): jnp.dot(far_ops[member], picked, preferred_element_type=jnp.float32)  31.7 us
    and x17, other arithmetic, interact(): picked = jnp.take(coef, located, axis=1)  9.92 us
    gather x40, other arithmetic  9.6 us
  transfers between devices with their start and end apart: 2, of which 0 were waited for; matrix products, arithmetic and copies ran while one was open for 15% of the time, Pallas kernels for 0%

commit v1 on v0

v1 whole, which is shorter than its diff:
```python
import functools

import jax
import jax.numpy as jnp
from jax import lax
from jax.experimental import pallas as pl
from jax.experimental.pallas import tpu as pltpu
from jax.sharding import PartitionSpec as P

MESH = pl.DeviceIdType.MESH
F32 = jnp.float32
BF16 = jnp.bfloat16


def nt(a, b):
    return lax.dot_general(a, b, (((1,), (1,)), ((), ())), preferred_element_type=F32)


def nn(a, b):
    return jnp.dot(a, b, preferred_element_type=F32)


def iota(shape, axis):
    return lax.broadcasted_iota(jnp.int32, shape, axis)


def take_rows(ref, start, rows, stride=1):
    parts = [ref[h, pl.ds(start, rows, stride=stride), :] for h in range(ref.shape[0])]
    return jnp.concatenate(parts, axis=1)


def put_rows(ref, start, rows, value, stride=1):
    for h in range(ref.shape[0]):
        ref[h, pl.ds(start, rows, stride=stride), :] = value[:, h * 128 : (h + 1) * 128]


def onehot(column, width, start=0):
    rows = column.shape[0]
    return jnp.where(iota((rows, width), 1) + start == column, 1.0, 0.0).astype(BF16)


def kernel(
    sizes,
    mult_h,
    comp_h,
    expd_h,
    octs_h,
    fars_h,
    l7_h,
    l6_h,
    l5_h,
    l4_h,
    l3_h,
    out_h,
    mult,
    comp,
    expd,
    octs,
    fars,
    l7,
    l6,
    l5,
    l4,
    l3,
    c7f,
    c6f,
    c4f,
    halo,
    small,
    every,
    own_pick,
    acc,
    d6,
    d7,
    outv,
    load_sem,
    out_sem,
    send_sem,
    recv_sem,
    all_send,
    all_recv,
):
    axes, counts, classes, nb4, nb3 = sizes
    n = counts[0] * counts[1]
    b7 = c7f.shape[1]
    b6 = b7 // 8
    b5 = b6 // 8
    per4 = 8 // b5
    block = b6 + 16
    me = lax.axis_index(axes[0]) * counts[1] + lax.axis_index(axes[1])

    def place(peer):
        return (peer // counts[1], peer % counts[1])

    loads = [
        pltpu.make_async_copy(src, dst, load_sem.at[k])
        for k, (src, dst) in enumerate(
            [
                (comp_h, comp),
                (mult_h, mult),
                (octs_h, octs),
                (l7_h, l7),
                (l6_h, l6),
                (l5_h, l5),
                (l4_h, l4),
                (l3_h, l3),
                (fars_h, fars),
                (expd_h, expd),
            ]
        )
    ]
    for load in loads:
        load.start()

    barrier = pltpu.get_barrier_semaphore()

    def greet(k, carry):
        pl.semaphore_signal(
            barrier, inc=1, device_id=place(lax.rem(me + k, n)), device_id_type=MESH
        )
        return carry

    lax.fori_loop(1, n, greet, 0)
    c6f[...] = jnp.zeros_like(c6f)
    c4f[...] = jnp.zeros_like(c4f)

    loads[0].wait()
    loads[1].wait()
    seven = nn(comp[...], mult[...]).astype(BF16).astype(F32).T
    put_rows(c7f, 0, b7, seven)
    halo[b7 : 2 * b7, :] = seven.astype(BF16)

    pl.semaphore_wait(barrier, n - 1)
    right = place(lax.rem(me + 1, n))
    left = place(lax.rem(me + n - 1, n))

    def halo_copy(ref, rows, slot, peer, index):
        return pltpu.make_async_remote_copy(
            src_ref=ref.at[pl.ds(rows, rows), :],
            dst_ref=ref.at[pl.ds(slot * rows, rows), :],
            send_sem=send_sem.at[index],
            recv_sem=recv_sem.at[index],
            device_id=peer,
            device_id_type=MESH,
        )

    halo_sends = [
        halo_copy(halo, b7, 0, right, 0),
        halo_copy(halo, b7, 2, left, 1),
    ]
    for copy in halo_sends:
        copy.start()

    loads[2].wait()
    total = jnp.zeros((b6, octs.shape[1]), F32)
    for o in range(8):
        total = total + nt(take_rows(c7f, o, b6, 8).astype(BF16), octs[o])
    six = total.astype(BF16)
    put_rows(c6f, 0, b6, six.astype(F32))
    total = jnp.zeros((16, octs.shape[1]), F32)
    for o in range(8):
        total = total + nt(take_rows(c6f, o, 16, 8).astype(BF16), octs[o])
    five = total.astype(BF16)
    small[block : block + b6, :] = six
    small[block + b6 : 2 * block, :] = five
    fivef = five.astype(F32)
    half = octs.shape[1] // 2
    tile = jnp.concatenate([fivef[0:b5, :half], fivef[0:b5, half:]], axis=0)
    mine = pl.ds(pl.multiple_of(me * 8, 8), 8)
    every[mine, :] = tile

    small_sends = [
        halo_copy(small, block, 0, right, 2),
        halo_copy(small, block, 2, left, 3),
    ]

    def spread(k, carry):
        pltpu.make_async_remote_copy(
            src_ref=every.at[mine, :],
            dst_ref=every.at[mine, :],
            send_sem=all_send,
            recv_sem=all_recv,
            device_id=place(lax.rem(me + k, n)),
            device_id_type=MESH,
        ).start()
        return carry

    lax.fori_loop(1, n, spread, 0)
    for copy in small_sends:
        copy.start()

    for k in range(3, 8):
        loads[k].wait()
    e7 = l7[...]
    p7 = jnp.where(e7 >= 0, e7 - (me * b7 - b7), -1).astype(F32).T.astype(jnp.int32)
    e6 = l6[...]
    p6 = e6 - (me * b6 - b6)
    p6 = p6 + jnp.where(p6 >= b6, block - b6, 0) + jnp.where(p6 >= 2 * b6, block - b6, 0)
    p6 = jnp.where(e6 >= 0, p6, -1).astype(F32)
    e5 = l5[...]
    p5 = e5 - (me * b5 - b5)
    p5 = p5 + b6 + jnp.where(p5 >= b5, block - b5, 0) + jnp.where(p5 >= 2 * b5, block - b5, 0)
    p5 = jnp.where(e5 >= 0, p5, -1).astype(F32)

    def column(row, rows):
        shape = (rows, row.shape[1])
        spread_row = jnp.where(iota(shape, 0) == iota(shape, 1), row, -1.0)
        return jnp.max(spread_row, axis=1, keepdims=True)

    for c in range(classes):
        own_pick[c] = nn(onehot(p7[:, c : c + 1], b7, b7), halo[b7 : 2 * b7, :]).astype(BF16)

    for copy in halo_sends + small_sends:
        copy.wait_recv()
    loads[8].wait()
    for c in range(classes):
        col = p7[:, c : c + 1]
        picked = own_pick[c].astype(F32)
        picked = picked + nn(onehot(col, b7, 0), halo[0:b7, :])
        picked = picked + nn(onehot(col, b7, 2 * b7), halo[2 * b7 : 3 * b7, :])
        cols = jnp.concatenate(
            [column(p6[c : c + 1, :], b6), column(p5[c : c + 1, :], 16)], axis=0
        ).astype(jnp.int32)
        lesser = nn(onehot(cols, 3 * block), small[...])
        both = jnp.concatenate([picked, lesser], axis=0).astype(BF16)
        if c == 0:
            acc[...] = nt(both, fars[c])
        else:
            acc[...] += nt(both, fars[c])

    rest = every.at[pl.ds(0, (n - 1) * 8), :]
    pltpu.make_async_copy(rest, rest, all_recv).wait()
    total = jnp.zeros((nb4, octs.shape[1]), F32)
    for o in range(8):
        at = (o // b5) * 8 + o % b5
        low = every[pl.ds(at, nb4, stride=8 * per4), :]
        high = every[pl.ds(at + b5, nb4, stride=8 * per4), :]
        total = total + nt(jnp.concatenate([low, high], axis=1).astype(BF16), octs[o])
    put_rows(c4f, 0, nb4, total.astype(BF16).astype(F32))
    rows3 = c4f.shape[1] // 8
    total = jnp.zeros((rows3, octs.shape[1]), F32)
    for o in range(8):
        total = total + nt(take_rows(c4f, o, rows3, 8).astype(BF16), octs[o])
    three = total.astype(BF16)
    t4 = me // per4
    t3 = t4 // 8

    def picked_one(entries, target, coef):
        lanes = iota(entries.shape, 1)
        chosen = jnp.where(lanes == target, entries, -1).astype(F32)
        col = jnp.max(chosen, axis=1, keepdims=True).astype(jnp.int32)
        return nn(onehot(col, coef.shape[0]), coef.astype(BF16))

    upper = jnp.concatenate(
        [picked_one(l4[...], t4, take_rows(c4f, 0, 8 * rows3)), picked_one(l3[...], t3, three)], axis=0
    )
    row = iota(upper.shape, 0) % classes
    total = jnp.zeros(upper.shape, F32)
    for c in range(classes):
        total = total + nt(jnp.where(row == c, upper, 0.0).astype(BF16), fars[c])
    far4 = 8.0 * jnp.sum(total[:classes], axis=0, keepdims=True)
    far3 = 16.0 * jnp.sum(total[classes:], axis=0, keepdims=True)

    wide = (16, octs.shape[1])
    down = nn(jnp.broadcast_to(far3, wide).astype(BF16), octs[t4 % 8])
    local4 = jnp.broadcast_to(far4 + down[0:1, :], wide)
    local5 = 4.0 * acc[b7 + b6 : b7 + block, :]
    first = (me % per4) * b5
    for k in range(b5):
        local5 = local5 + nn(
            jnp.where(iota(wide, 0) == k, local4, 0.0).astype(BF16), octs[first + k]
        )
    local5 = local5.astype(BF16)
    for o in range(8):
        put_rows(d6, o, 8, nn(local5, octs[o])[0:8, :], 8)
    local6 = (2.0 * acc[b7 : b7 + b6, :] + take_rows(d6, 0, b6)).astype(BF16)
    for o in range(8):
        put_rows(d7, o, b6, nn(local6, octs[o]), 8)
    local7 = (acc[0:b7, :] + take_rows(d7, 0, b7)).astype(BF16)

    loads[9].wait()
    surface = expd.shape[0]
    step = 304
    stores = []
    for k, start in enumerate(range(0, surface, step)):
        stop = min(start + step, surface)
        outv[start:stop, :] = nt(expd[start:stop, :], local7)
        store = pltpu.make_async_copy(
            outv.at[pl.ds(start, stop - start), :],
            out_h.at[pl.ds(start, stop - start), :],
            out_sem.at[k],
        )
        store.start()
        stores.append(store)
    for copy in halo_sends + small_sends:
        copy.wait_send()
    pltpu.make_async_copy(rest, rest, all_send).wait()
    for store in stores:
        store.wait()


def on_device(axes, counts, *args):
    mult, comp, expd, octs, fars, l7, l6, l5, l4, l3 = args
    n = counts[0] * counts[1]
    b7, b6, b5 = l7.shape[1], l6.shape[1], l5.shape[1]
    nb4, nb3 = l4.shape[1], l3.shape[1]
    classes, r = fars.shape[0], fars.shape[1]
    if b6 * 8 != b7 or b5 * 8 != b6 or b5 != 4:
        raise ValueError("unsupported sizes")
    block = b6 + 16
    rows3 = max(16, nb3)
    scratch = [pltpu.VMEM(a.shape, a.dtype) for a in args]
    scratch += [
        pltpu.VMEM((r // 128, b7, 128), F32),
        pltpu.VMEM((r // 128, 128, 128), F32),
        pltpu.VMEM((r // 128, rows3 * 8, 128), F32),
        pltpu.VMEM((3 * b7, r), BF16),
        pltpu.VMEM((3 * block, r), BF16),
        pltpu.VMEM((n * 8, r // 2), F32),
        pltpu.VMEM((classes, b7, r), BF16),
        pltpu.VMEM((b7 + block, r), F32),
        pltpu.VMEM((r // 128, 64, 128), F32),
        pltpu.VMEM((r // 128, b7, 128), F32),
        pltpu.VMEM((expd.shape[0], b7), F32),
        pltpu.SemaphoreType.DMA((10,)),
        pltpu.SemaphoreType.DMA((3,)),
        pltpu.SemaphoreType.DMA((4,)),
        pltpu.SemaphoreType.DMA((4,)),
        pltpu.SemaphoreType.DMA,
        pltpu.SemaphoreType.DMA,
    ]
    return pl.pallas_call(
        functools.partial(kernel, (axes, counts, classes, nb4, nb3)),
        out_shape=jax.ShapeDtypeStruct((expd.shape[0], b7), F32),
        in_specs=[pl.BlockSpec(memory_space=pl.ANY)] * len(args),
        out_specs=pl.BlockSpec(memory_space=pl.ANY),
        scratch_shapes=scratch,
        compiler_params=pltpu.CompilerParams(
            collective_id=0, has_side_effects=True, vmem_limit_bytes=50 * 1024 * 1024
        ),
    )(*args)


def solution(mesh):
    axes = tuple(mesh.axis_names)
    counts = tuple(mesh.shape[a] for a in axes)
    cut = P(None, axes)
    return jax.shard_map(
        functools.partial(on_device, axes, counts),
        mesh=mesh,
        in_specs=(cut, P(), P(), P(), P(), cut, cut, cut, P(), P()),
        out_specs=cut,
        check_vma=False,
    )
```

time: 235 us -> 30.8 us (0.13)
  the two profiles are of different devices: /device:TPU:0 before, /device:TPU:1 now
where the time goes in v1:
time: 30.8 us; the launch traced here: 30.3 us
  Pallas kernels  21.2 us (69%)
  local copies, waits for them, and re-layouts  9.06 us (29%)
    pallas_call x1, Pallas kernels, on_device(): pl.pallas_call(functools.partial(kernel, (axes, counts, classes, nb4, nb3...  21.2 us
    unnamed x16, local copies, waits for them, and re-layouts  9.06 us

profile of v1, /device:TPU:1, one launch (start us, length us, event | category | flops | bytes accessed | tf_op | source)
XLA Modules:
  0.0 30.3 jit_solution(8421988106283535134)
XLA Ops:
  0.0 0.8 %copy.12.l5_h = s32[16,4]{1,0:T(8,128)S(1)} copy(s32[16,4]{0,1:T(4,128)} %param.17) | data formatting | bytes 512 | tf_op args[7]
  0.8 0.8 %copy.13.l3_h = s32[16,2]{1,0:T(8,128)S(1)} copy(s32[16,2]{0,1:T(2,128)} %param.19) | data formatting | bytes 256 | tf_op args[9]
  1.5 1.3 %copy.11.comp_h = bf16[256,888]{1,0:T(8,128)(2,1)S(1)} copy(bf16[256,888]{0,1:T(8,128)(2,1)} %param.11) | data formatting | bytes 909312 | tf_op args[1]
  2.8 0.0 copy-start
  2.8 1.2 %copy-done = bf16[8,256,256]{2,1,0:T(8,128)(2,1)S(1)} copy-done((bf16[8,256,256]{2,1,0:T(8,128)(2,1)S(1)}, bf16[8,256,256]{2,1,0:T(8,128)(2,1)}, u32[]{:S(2)}) %copy-start) | copy-done | bytes 1048600
  4.0 0.0 copy-start.1
  4.0 1.0 %copy-done.1 = bf16[888,256]{1,0:T(8,128)(2,1)S(1)} copy-done((bf16[888,256]{1,0:T(8,128)(2,1)S(1)}, bf16[888,256]{1,0:T(8,128)(2,1)}, u32[]{:S(2)}) %copy-start.1) | copy-done | bytes 454680
  5.0 0.0 copy-start.2
  5.0 1.0 %copy-done.2 = bf16[888,256]{1,0:T(8,128)(2,1)S(1)} copy-done((bf16[888,256]{1,0:T(8,128)(2,1)S(1)}, bf16[888,256]{1,0:T(8,128)(2,1)}, u32[]{:S(2)}) %copy-start.2) | copy-done | bytes 454680
  6.0 0.0 copy-start.3
  6.0 0.7 %copy-done.3 = s32[16,256]{1,0:T(8,128)S(1)} copy-done((s32[16,256]{1,0:T(8,128)S(1)}, s32[16,256]{1,0:T(8,128)}, u32[]{:S(2)}) %copy-start.3) | copy-done | bytes 16408
  6.8 0.0 copy-start.4
  6.8 0.7 %copy-done.4 = s32[16,32]{1,0:T(8,128)S(1)} copy-done((s32[16,32]{1,0:T(8,128)S(1)}, s32[16,32]{1,0:T(8,128)}, u32[]{:S(2)}) %copy-start.4) | copy-done | bytes 2072
  7.5 0.0 copy-start.5
  7.5 0.7 %copy-done.5 = s32[16,16]{1,0:T(8,128)S(1)} copy-done((s32[16,16]{1,0:T(8,128)S(1)}, s32[16,16]{1,0:T(8,128)}, u32[]{:S(2)}) %copy-start.5) | copy-done | bytes 1048
  8.2 21.2 %shard_map.100 = f32[888,256]{1,0:T(8,128)S(1)} custom-call(bf16[888,256]{1,0:T(8,128)(2,1)S(1)} %copy-done.1, bf16[256,888]{1,0:T(8,128)(2,1)S(1)} %copy.11.comp_h, bf16[888,256]{1,0:T(8,128)(2,1)S(1)} %copy-done.2, bf16[8,256,256]{2,1,0:T(8,128)(2,1)S(1)} %copy-done, bf16[16,256,256]{2,1,0:T(8,128)(2,1)} %fars_h.1, s32[16,256]{1,0:T(8,128)S(1)} %copy-done.3, ...), custom_call_target="tpu_custom_call" | custom-call | tf_op jit(solution)/shard_map/pallas_call | solution.py:332
  29.4 0.9 %copy.15 = f32[888,256]{1,0:T(8,128)} copy(f32[888,256]{1,0:T(8,128)S(1)} %shard_map.100) | data formatting | bytes 1818624
Async XLA Ops:
  2.8 1.2 %copy-start = (bf16[8,256,256]{2,1,0:T(8,128)(2,1)S(1)}, bf16[8,256,256]{2,1,0:T(8,128)(2,1)}, u32[]{:S(2)}) copy-start(bf16[8,256,256]{2,1,0:T(8,128)(2,1)} %octs_h.1) | copy-start | bytes 3145732
  4.0 1.0 %copy-start.1 = (bf16[888,256]{1,0:T(8,128)(2,1)S(1)}, bf16[888,256]{1,0:T(8,128)(2,1)}, u32[]{:S(2)}) copy-start(bf16[888,256]{1,0:T(8,128)(2,1)} %mult_h.1) | copy-start | bytes 1363972
  5.0 1.0 %copy-start.2 = (bf16[888,256]{1,0:T(8,128)(2,1)S(1)}, bf16[888,256]{1,0:T(8,128)(2,1)}, u32[]{:S(2)}) copy-start(bf16[888,256]{1,0:T(8,128)(2,1)} %expd_h.1) | copy-start | bytes 1363972
  6.0 0.7 %copy-start.3 = (s32[16,256]{1,0:T(8,128)S(1)}, s32[16,256]{1,0:T(8,128)}, u32[]{:S(2)}) copy-start(s32[16,256]{1,0:T(8,128)} %l7_h.1) | copy-start | bytes 49156
  6.8 0.7 %copy-start.4 = (s32[16,32]{1,0:T(8,128)S(1)}, s32[16,32]{1,0:T(8,128)}, u32[]{:S(2)}) copy-start(s32[16,32]{1,0:T(8,128)} %l6_h.1) | copy-start | bytes 6148
  7.5 0.7 %copy-start.5 = (s32[16,16]{1,0:T(8,128)S(1)}, s32[16,16]{1,0:T(8,128)}, u32[]{:S(2)}) copy-start(s32[16,16]{1,0:T(8,128)} %l4_h.1) | copy-start | bytes 3076

commit v2 on v1

--- a/solution.py
+++ b/solution.py
@@ -16,6 +16,10 @@
     return lax.dot_general(a, b, (((1,), (1,)), ((), ())), preferred_element_type=F32)
 
 
+def tn(a, b):
+    return lax.dot_general(a, b, (((0,), (0,)), ((), ())), preferred_element_type=F32)
+
+
 def nn(a, b):
     return jnp.dot(a, b, preferred_element_type=F32)
 
@@ -37,6 +41,12 @@
 def onehot(column, width, start=0):
     rows = column.shape[0]
     return jnp.where(iota((rows, width), 1) + start == column, 1.0, 0.0).astype(BF16)
+
+
+def column(row, rows):
+    shape = (rows, row.shape[1])
+    spread_row = jnp.where(iota(shape, 0) == iota(shape, 1), row, -1.0)
+    return jnp.max(spread_row, axis=1, keepdims=True)
 
 
 def kernel(
@@ -51,7 +61,7 @@
     l5_h,
     l4_h,
     l3_h,
-    out_h,
+    outv,
     mult,
     comp,
     expd,
@@ -65,16 +75,17 @@
     c7f,
     c6f,
     c4f,
+    own,
     halo,
     small,
     every,
     own_pick,
+    hot,
+    hot_small,
     acc,
     d6,
     d7,
-    outv,
     load_sem,
-    out_sem,
     send_sem,
     recv_sem,
     all_send,
@@ -109,7 +120,7 @@
             ]
         )
     ]
-    for load in loads:
+    for load in loads[:8]:
         load.start()
 
     barrier = pltpu.get_barrier_semaphore()
@@ -126,17 +137,19 @@
 
     loads[0].wait()
     loads[1].wait()
-    seven = nn(comp[...], mult[...]).astype(BF16).astype(F32).T
-    put_rows(c7f, 0, b7, seven)
-    halo[b7 : 2 * b7, :] = seven.astype(BF16)
+    loads[8].start()
+    loads[9].start()
+    seven = tn(mult[...], comp[...]).astype(BF16)
+    own[...] = seven
+    put_rows(c7f, 0, b7, seven.astype(F32))
 
     pl.semaphore_wait(barrier, n - 1)
     right = place(lax.rem(me + 1, n))
     left = place(lax.rem(me + n - 1, n))
 
-    def halo_copy(ref, rows, slot, peer, index):
+    def halo_copy(src, ref, rows, slot, peer, index):
         return pltpu.make_async_remote_copy(
-            src_ref=ref.at[pl.ds(rows, rows), :],
+            src_ref=src,
             dst_ref=ref.at[pl.ds(slot * rows, rows), :],
             send_sem=send_sem.at[index],
             recv_sem=recv_sem.at[index],
@@ -145,8 +158,8 @@
         )
 
     halo_sends = [
-        halo_copy(halo, b7, 0, right, 0),
-        halo_copy(halo, b7, 2, left, 1),
+        halo_copy(own, halo, b7, 0, right, 0),
+        halo_copy(own, halo, b7, 1, left, 1),
     ]
     for copy in halo_sends:
         copy.start()
@@ -170,8 +183,8 @@
     every[mine, :] = tile
 
     small_sends = [
-        halo_copy(small, block, 0, right, 2),
-        halo_copy(small, block, 2, left, 3),
+        halo_copy(small.at[pl.ds(block, block), :], small, block, 0, right, 2),
+        halo_copy(small.at[pl.ds(block, block), :], small, block, 2, left, 3),
     ]
 
     def spread(k, carry):
@@ -200,34 +213,20 @@
     e5 = l5[...]
     p5 = e5 - (me * b5 - b5)
     p5 = p5 + b6 + jnp.where(p5 >= b5, block - b5, 0) + jnp.where(p5 >= 2 * b5, block - b5, 0)
-    p5 = jnp.where(e5 >= 0, p5, -1).astype(F32)
-
-    def column(row, rows):
-        shape = (rows, row.shape[1])
-        spread_row = jnp.where(iota(shape, 0) == iota(shape, 1), row, -1.0)
-        return jnp.max(spread_row, axis=1, keepdims=True)
-
-    for c in range(classes):
-        own_pick[c] = nn(onehot(p7[:, c : c + 1], b7, b7), halo[b7 : 2 * b7, :]).astype(BF16)
-
-    for copy in halo_sends + small_sends:
-        copy.wait_recv()
-    loads[8].wait()
+    p5 = jnp.where(e5 >= 0, p5, -1)
+    p5 = jnp.concatenate([p5, jnp.full((16 - b5, classes), -1, jnp.int32)], axis=0)
+
     for c in range(classes):
         col = p7[:, c : c + 1]
-        picked = own_pick[c].astype(F32)
-        picked = picked + nn(onehot(col, b7, 0), halo[0:b7, :])
-        picked = picked + nn(onehot(col, b7, 2 * b7), halo[2 * b7 : 3 * b7, :])
+        own_pick[c] = nn(onehot(col, b7, b7), own[...]).astype(BF16)
+        hot[c, :, 0:b7] = onehot(col, b7, 0)
+        hot[c, :, b7 : 2 * b7] = onehot(col, b7, 2 * b7)
         cols = jnp.concatenate(
-            [column(p6[c : c + 1, :], b6), column(p5[c : c + 1, :], 16)], axis=0
-        ).astype(jnp.int32)
-        lesser = nn(onehot(cols, 3 * block), small[...])
-        both = jnp.concatenate([picked, lesser], axis=0).astype(BF16)
-        if c == 0:
-            acc[...] = nt(both, fars[c])
-        else:
-            acc[...] += nt(both, fars[c])
-
+            [column(p6[c : c + 1, :], b6).astype(jnp.int32), p5[:, c : c + 1]], axis=0
+        )
+        hot_small[c] = onehot(cols, 3 * block)
+
+    loads[8].wait()
     rest = every.at[pl.ds(0, (n - 1) * 8), :]
     pltpu.make_async_copy(rest, rest, all_recv).wait()
     total = jnp.zeros((nb4, octs.shape[1]), F32)
@@ -245,14 +244,15 @@
     t4 = me // per4
     t3 = t4 // 8
 
-    def picked_one(entries, target, coef):
-        lanes = iota(entries.shape, 1)
-        chosen = jnp.where(lanes == target, entries, -1).astype(F32)
-        col = jnp.max(chosen, axis=1, keepdims=True).astype(jnp.int32)
-        return nn(onehot(col, coef.shape[0]), coef.astype(BF16))
-
+    e4 = l4[...]
+    chosen4 = jnp.where(iota(e4.shape, 1) == t4, e4, -1).astype(F32)
+    chosen4 = jnp.max(chosen4, axis=1, keepdims=True).astype(jnp.int32)
+    e3 = l3[...]
+    chosen3 = jnp.where(iota(e3.shape, 0) == t3, e3, -1).astype(F32)
+    chosen3 = column(jnp.max(chosen3, axis=0, keepdims=True), classes).astype(jnp.int32)
+    four = take_rows(c4f, 0, 8 * rows3).astype(BF16)
     upper = jnp.concatenate(
-        [picked_one(l4[...], t4, take_rows(c4f, 0, 8 * rows3)), picked_one(l3[...], t3, three)], axis=0
+        [nn(onehot(chosen4, 8 * rows3), four), nn(onehot(chosen3, rows3), three)], axis=0
     )
     row = iota(upper.shape, 0) % classes
     total = jnp.zeros(upper.shape, F32)
@@ -264,13 +264,24 @@
     wide = (16, octs.shape[1])
     down = nn(jnp.broadcast_to(far3, wide).astype(BF16), octs[t4 % 8])
     local4 = jnp.broadcast_to(far4 + down[0:1, :], wide)
-    local5 = 4.0 * acc[b7 + b6 : b7 + block, :]
+    local5 = jnp.zeros(wide, F32)
     first = (me % per4) * b5
     for k in range(b5):
         local5 = local5 + nn(
             jnp.where(iota(wide, 0) == k, local4, 0.0).astype(BF16), octs[first + k]
         )
-    local5 = local5.astype(BF16)
+    for copy in halo_sends + small_sends:
+        copy.wait_recv()
+    for c in range(classes):
+        picked = nn(hot[c], halo[...]) + own_pick[c].astype(F32)
+        lesser = nn(hot_small[c], small[...])
+        both = jnp.concatenate([picked, lesser], axis=0).astype(BF16)
+        if c == 0:
+            acc[...] = nt(both, fars[c])
+        else:
+            acc[...] += nt(both, fars[c])
+
+    local5 = (4.0 * acc[b7 + b6 : b7 + block, :] + local5).astype(BF16)
     for o in range(8):
         put_rows(d6, o, 8, nn(local5, octs[o])[0:8, :], 8)
     local6 = (2.0 * acc[b7 : b7 + b6, :] + take_rows(d6, 0, b6)).astype(BF16)
@@ -281,26 +292,17 @@
     loads[9].wait()
     surface = expd.shape[0]
     step = 304
-    stores = []
-    for k, start in enumerate(range(0, surface, step)):
+    for start in range(0, surface, step):
         stop = min(start + step, surface)
         outv[start:stop, :] = nt(expd[start:stop, :], local7)
-        store = pltpu.make_async_copy(
-            outv.at[pl.ds(start, stop - start), :],
-            out_h.at[pl.ds(start, stop - start), :],
-            out_sem.at[k],
-        )
-        store.start()
-        stores.append(store)
     for copy in halo_sends + small_sends:
         copy.wait_send()
     pltpu.make_async_copy(rest, rest, all_send).wait()
-    for store in stores:
-        store.wait()
 
 
 def on_device(axes, counts, *args):
     mult, comp, expd, octs, fars, l7, l6, l5, l4, l3 = args
+    args = (mult, comp.T, expd, octs, fars, l7, l6, l5.T, l4, l3.T)
     n = counts[0] * counts[1]
     b7, b6, b5 = l7.shape[1], l6.shape[1], l5.shape[1]
     nb4, nb3 = l4.shape[1], l3.shape[1]
@@ -314,16 +316,17 @@
         pltpu.VMEM((r // 128, b7, 128), F32),
         pltpu.VMEM((r // 128, 128, 128), F32),
         pltpu.VMEM((r // 128, rows3 * 8, 128), F32),
-        pltpu.VMEM((3 * b7, r), BF16),
+        pltpu.VMEM((b7, r), BF16),
+        pltpu.VMEM((2 * b7, r), BF16),
         pltpu.VMEM((3 * block, r), BF16),
         pltpu.VMEM((n * 8, r // 2), F32),
         pltpu.VMEM((classes, b7, r), BF16),
+        pltpu.VMEM((classes, b7, 2 * b7), BF16),
+        pltpu.VMEM((classes, block, 3 * block), BF16),
         pltpu.VMEM((b7 + block, r), F32),
         pltpu.VMEM((r // 128, 64, 128), F32),
         pltpu.VMEM((r // 128, b7, 128), F32),
-        pltpu.VMEM((expd.shape[0], b7), F32),
         pltpu.SemaphoreType.DMA((10,)),
-        pltpu.SemaphoreType.DMA((3,)),
         pltpu.SemaphoreType.DMA((4,)),
         pltpu.SemaphoreType.DMA((4,)),
         pltpu.SemaphoreType.DMA,
@@ -332,11 +335,11 @@
     return pl.pallas_call(
         functools.partial(kernel, (axes, counts, classes, nb4, nb3)),
         out_shape=jax.ShapeDtypeStruct((expd.shape[0], b7), F32),
-        in_specs=[pl.BlockSpec(memory_space=pl.ANY)] * len(args),
-        out_specs=pl.BlockSpec(memory_space=pl.ANY),
+        in_specs=[pl.BlockSpec(memory_space=pltpu.HBM)] * len(args),
+        out_specs=pl.BlockSpec(memory_space=pltpu.VMEM),
         scratch_shapes=scratch,
         compiler_params=pltpu.CompilerParams(
-            collective_id=0, has_side_effects=True, vmem_limit_bytes=50 * 1024 * 1024
+            collective_id=0, has_side_effects=True, vmem_limit_bytes=60 * 1024 * 1024
         ),
     )(*args)
 

time: 30.8 us -> 23.7 us (0.77)
  the two profiles are of different devices: /device:TPU:1 before, /device:TPU:0 now
where the time goes in v2:
time: 23.7 us; the launch traced here: 23.5 us
  Pallas kernels  21.3 us (90%)
  local copies, waits for them, and re-layouts  2.15 us (9%)
    pallas_call x1, Pallas kernels, on_device(): pl.pallas_call(functools.partial(kernel, (axes, counts, classes, nb4, nb3...  21.3 us
    unnamed x1, local copies, waits for them, and re-layouts  2.15 us

profile of v2, /device:TPU:0, one launch (start us, length us, event | category | flops | bytes accessed | tf_op | source)
XLA Modules:
  0.0 23.5 jit_solution(15105300650753455651)
XLA Ops:
  0.0 21.3 %shard_map.100 = f32[888,256]{1,0:T(8,128)} custom-call(bf16[888,256]{1,0:T(8,128)(2,1)} %mult_h.1, bf16[888,256]{1,0:T(8,128)(2,1)} %bitcast.3, bf16[888,256]{1,0:T(8,128)(2,1)} %expd_h.1, bf16[8,256,256]{2,1,0:T(8,128)(2,1)} %octs_h.1, bf16[16,256,256]{2,1,0:T(8,128)(2,1)} %fars_h.1, s32[16,256]{1,0:T(8,128)} %l7_h.1, s32[16,32]{1,0:T(8,128)} %l6_h.1, ...), custom_call_target="tpu_custom_call" | custom-call | tf_op jit(solution)/shard_map/pallas_call | solution.py:335
  21.3 2.2 %copy.12 = f32[888,256]{1,0:T(8,128)} copy(f32[888,256]{1,0:T(8,128)} %shard_map.100) | data formatting | bytes 1818624

commit v3 on v2

--- a/solution.py
+++ b/solution.py
@@ -134,6 +134,12 @@
     lax.fori_loop(1, n, greet, 0)
     c6f[...] = jnp.zeros_like(c6f)
     c4f[...] = jnp.zeros_like(c4f)
+    rows3 = c4f.shape[1] // 8
+    base4 = 3 * block
+    base3 = base4 + nb4
+    depth = small.shape[0]
+    t4 = me // per4
+    t3 = t4 // 8
 
     loads[0].wait()
     loads[1].wait()
@@ -216,78 +222,92 @@
     p5 = jnp.where(e5 >= 0, p5, -1)
     p5 = jnp.concatenate([p5, jnp.full((16 - b5, classes), -1, jnp.int32)], axis=0)
 
+    e4 = l4[...]
+    p4 = jnp.where(iota(e4.shape, 1) == t4, e4, -1).astype(F32)
+    p4 = jnp.max(p4, axis=1, keepdims=True).astype(jnp.int32)
+    p4 = jnp.where(p4 >= 0, p4 + base4, -1)
+    e3 = l3[...]
+    p3 = jnp.where(iota(e3.shape, 0) == t3, e3, -1).astype(F32)
+    p3 = column(jnp.max(p3, axis=0, keepdims=True), classes).astype(jnp.int32)
+    p3 = jnp.where(p3 >= 0, p3 + base3, -1)
+    row = iota((16, 1), 0)
+
     for c in range(classes):
         col = p7[:, c : c + 1]
         own_pick[c] = nn(onehot(col, b7, b7), own[...]).astype(BF16)
         hot[c, :, 0:b7] = onehot(col, b7, 0)
         hot[c, :, b7 : 2 * b7] = onehot(col, b7, 2 * b7)
-        cols = jnp.concatenate(
-            [column(p6[c : c + 1, :], b6).astype(jnp.int32), p5[:, c : c + 1]], axis=0
-        )
-        hot_small[c] = onehot(cols, 3 * block)
+        tail = jnp.where(row == b5, p4[c : c + 1, :], p5[:, c : c + 1])
+        tail = jnp.where(row == b5 + 1, p3[c : c + 1, :], tail)
+        cols = jnp.concatenate([column(p6[c : c + 1, :], b6).astype(jnp.int32), tail], axis=0)
+        hot_small[c] = onehot(cols, depth)
 
     loads[8].wait()
     rest = every.at[pl.ds(0, (n - 1) * 8), :]
     pltpu.make_async_copy(rest, rest, all_recv).wait()
-    total = jnp.zeros((nb4, octs.shape[1]), F32)
-    for o in range(8):
-        at = (o // b5) * 8 + o % b5
-        low = every[pl.ds(at, nb4, stride=8 * per4), :]
-        high = every[pl.ds(at + b5, nb4, stride=8 * per4), :]
-        total = total + nt(jnp.concatenate([low, high], axis=1).astype(BF16), octs[o])
-    put_rows(c4f, 0, nb4, total.astype(BF16).astype(F32))
-    rows3 = c4f.shape[1] // 8
-    total = jnp.zeros((rows3, octs.shape[1]), F32)
-    for o in range(8):
-        total = total + nt(take_rows(c4f, o, rows3, 8).astype(BF16), octs[o])
-    three = total.astype(BF16)
-    t4 = me // per4
-    t3 = t4 // 8
-
-    e4 = l4[...]
-    chosen4 = jnp.where(iota(e4.shape, 1) == t4, e4, -1).astype(F32)
-    chosen4 = jnp.max(chosen4, axis=1, keepdims=True).astype(jnp.int32)
-    e3 = l3[...]
-    chosen3 = jnp.where(iota(e3.shape, 0) == t3, e3, -1).astype(F32)
-    chosen3 = column(jnp.max(chosen3, axis=0, keepdims=True), classes).astype(jnp.int32)
-    four = take_rows(c4f, 0, 8 * rows3).astype(BF16)
-    upper = jnp.concatenate(
-        [nn(onehot(chosen4, 8 * rows3), four), nn(onehot(chosen3, rows3), three)], axis=0
-    )
-    row = iota(upper.shape, 0) % classes
-    total = jnp.zeros(upper.shape, F32)
-    for c in range(classes):
-        total = total + nt(jnp.where(row == c, upper, 0.0).astype(BF16), fars[c])
-    far4 = 8.0 * jnp.sum(total[:classes], axis=0, keepdims=True)
-    far3 = 16.0 * jnp.sum(total[classes:], axis=0, keepdims=True)
-
-    wide = (16, octs.shape[1])
-    down = nn(jnp.broadcast_to(far3, wide).astype(BF16), octs[t4 % 8])
-    local4 = jnp.broadcast_to(far4 + down[0:1, :], wide)
-    local5 = jnp.zeros(wide, F32)
-    first = (me % per4) * b5
-    for k in range(b5):
-        local5 = local5 + nn(
-            jnp.where(iota(wide, 0) == k, local4, 0.0).astype(BF16), octs[first + k]
-        )
     for copy in halo_sends + small_sends:
         copy.wait_recv()
+
+    def coarser():
+        total = jnp.zeros((nb4, octs.shape[1]), F32)
+        for o in range(8):
+            at = (o // b5) * 8 + o % b5
+            low = every[pl.ds(at, nb4, stride=8 * per4), :]
+            high = every[pl.ds(at + b5, nb4, stride=8 * per4), :]
+            total = total + nt(jnp.concatenate([low, high], axis=1).astype(BF16), octs[o])
+            if o % 4 == 3:
+                yield
+        four = total.astype(BF16)
+        put_rows(c4f, 0, nb4, four.astype(F32))
+        small[base4 : base4 + nb4, :] = four
+        total = jnp.zeros((rows3, octs.shape[1]), F32)
+        for o in range(8):
+            total = total + nt(take_rows(c4f, o, rows3, 8).astype(BF16), octs[o])
+            if o % 4 == 3:
+                yield
+        small[base3 : base3 + rows3, :] = total.astype(BF16)
+        far = jnp.zeros((block, octs.shape[1]), F32)
+        for c in range(classes):
+            lesser = nn(hot_small[c], small[...]).astype(BF16)
+            far = far + nt(lesser, fars[c])
+            if c % 4 == 3:
+                yield
+        far6, far5 = 2.0 * far[0:b6, :], 4.0 * far[b6:block, :]
+        far4 = 8.0 * far[b6 + b5 : b6 + b5 + 1, :]
+        far3 = 16.0 * far[b6 + b5 + 1 : b6 + b5 + 2, :]
+        wide = (16, octs.shape[1])
+        down = nn(jnp.broadcast_to(far3, wide).astype(BF16), octs[t4 % 8])
+        local4 = jnp.broadcast_to(far4 + down[0:1, :], wide)
+        yield
+        local5 = far5
+        first = (me % per4) * b5
+        for k in range(b5):
+            local5 = local5 + nn(
+                jnp.where(iota(wide, 0) == k, local4, 0.0).astype(BF16), octs[first + k]
+            )
+        local5 = local5.astype(BF16)
+        yield
+        for o in range(8):
+            put_rows(d6, o, 8, nn(local5, octs[o])[0:8, :], 8)
+        local6 = (far6 + take_rows(d6, 0, b6)).astype(BF16)
+        yield
+        for o in range(8):
+            put_rows(d7, o, b6, nn(local6, octs[o]), 8)
+            if o % 4 == 3:
+                yield
+
+    chain = coarser()
+    next(chain, None)
     for c in range(classes):
+        next(chain, None)
         picked = nn(hot[c], halo[...]) + own_pick[c].astype(F32)
-        lesser = nn(hot_small[c], small[...])
-        both = jnp.concatenate([picked, lesser], axis=0).astype(BF16)
         if c == 0:
-            acc[...] = nt(both, fars[c])
+            acc[...] = nt(picked.astype(BF16), fars[c])
         else:
-            acc[...] += nt(both, fars[c])
-
-    local5 = (4.0 * acc[b7 + b6 : b7 + block, :] + local5).astype(BF16)
-    for o in range(8):
-        put_rows(d6, o, 8, nn(local5, octs[o])[0:8, :], 8)
-    local6 = (2.0 * acc[b7 : b7 + b6, :] + take_rows(d6, 0, b6)).astype(BF16)
-    for o in range(8):
-        put_rows(d7, o, b6, nn(local6, octs[o]), 8)
-    local7 = (acc[0:b7, :] + take_rows(d7, 0, b7)).astype(BF16)
+            acc[...] += nt(picked.astype(BF16), fars[c])
+    for _ in chain:
+        pass
+    local7 = (acc[...] + take_rows(d7, 0, b7)).astype(BF16)
 
     loads[9].wait()
     surface = expd.shape[0]
@@ -307,10 +327,11 @@
     b7, b6, b5 = l7.shape[1], l6.shape[1], l5.shape[1]
     nb4, nb3 = l4.shape[1], l3.shape[1]
     classes, r = fars.shape[0], fars.shape[1]
-    if b6 * 8 != b7 or b5 * 8 != b6 or b5 != 4:
+    if b6 * 8 != b7 or b5 * 8 != b6 or b5 != 4 or nb4 % 16:
         raise ValueError("unsupported sizes")
     block = b6 + 16
     rows3 = max(16, nb3)
+    depth = 3 * block + nb4 + rows3
     scratch = [pltpu.VMEM(a.shape, a.dtype) for a in args]
     scratch += [
         pltpu.VMEM((r // 128, b7, 128), F32),
@@ -318,12 +339,12 @@
         pltpu.VMEM((r // 128, rows3 * 8, 128), F32),
         pltpu.VMEM((b7, r), BF16),
         pltpu.VMEM((2 * b7, r), BF16),
-        pltpu.VMEM((3 * block, r), BF16),
+        pltpu.VMEM((depth, r), BF16),
         pltpu.VMEM((n * 8, r // 2), F32),
         pltpu.VMEM((classes, b7, r), BF16),
         pltpu.VMEM((classes, b7, 2 * b7), BF16),
-        pltpu.VMEM((classes, block, 3 * block), BF16),
-        pltpu.VMEM((b7 + block, r), F32),
+        pltpu.VMEM((classes, block, depth), BF16),
+        pltpu.VMEM((b7, r), F32),
         pltpu.VMEM((r // 128, 64, 128), F32),
         pltpu.VMEM((r // 128, b7, 128), F32),
         pltpu.SemaphoreType.DMA((10,)),
@@ -334,14 +355,14 @@
     ]
     return pl.pallas_call(
         functools.partial(kernel, (axes, counts, classes, nb4, nb3)),
-        out_shape=jax.ShapeDtypeStruct((expd.shape[0], b7), F32),
+        out_shape=pltpu.VMEM((expd.shape[0], b7), F32),
         in_specs=[pl.BlockSpec(memory_space=pltpu.HBM)] * len(args),
         out_specs=pl.BlockSpec(memory_space=pltpu.VMEM),
         scratch_shapes=scratch,
         compiler_params=pltpu.CompilerParams(
-            collective_id=0, has_side_effects=True, vmem_limit_bytes=60 * 1024 * 1024
+            collective_id=0, has_side_effects=True, vmem_limit_bytes=50 * 1024 * 1024
         ),
-    )(*args)
+    )(*[pltpu.with_memory_space_constraint(a, pltpu.HBM) for a in args])
 
 
 def solution(mesh):

time: 23.7 us -> 20.7 us (0.87)
  Pallas kernels: 21.3 us -> 19.7 us
  local copies, waits for them, and re-layouts: 2.15 us -> 0.92 us
    pallas_call x1, Pallas kernels: 21.3 us -> 19.7 us  [on_device(): pl.pallas_call(functools.partial(kernel, (axes, counts, classes, nb4, nb3...]
    unnamed x1, local copies, waits for them, and re-layouts: 2.15 us -> 0.92 us
where the time goes in v3:
time: 20.7 us; the launch traced here: 20.6 us
  Pallas kernels  19.7 us (95%)
  local copies, waits for them, and re-layouts  0.92 us (4%)
    pallas_call x1, Pallas kernels, on_device(): pl.pallas_call(functools.partial(kernel, (axes, counts, classes, nb4, nb3...  19.7 us
    unnamed x1, local copies, waits for them, and re-layouts  0.92 us

profile of v3, /device:TPU:0, one launch (start us, length us, event | category | flops | bytes accessed | tf_op | source)
XLA Modules:
  0.0 20.6 jit_solution(11870282646942160692)
XLA Ops:
  0.0 19.7 %shard_map.100 = f32[888,256]{1,0:T(8,128)S(1)} custom-call(bf16[888,256]{1,0:T(8,128)(2,1)} %mult_h.1, bf16[888,256]{1,0:T(8,128)(2,1)} %bitcast.3, bf16[888,256]{1,0:T(8,128)(2,1)} %expd_h.1, bf16[8,256,256]{2,1,0:T(8,128)(2,1)} %octs_h.1, bf16[16,256,256]{2,1,0:T(8,128)(2,1)} %fars_h.1, s32[16,256]{1,0:T(8,128)} %l7_h.1, s32[16,32]{1,0:T(8,128)} %l6_h.1, ...), custom_call_target="tpu_custom_call" | custom-call | tf_op jit(solution)/shard_map/pallas_call | solution.py:356
  19.7 0.9 %copy.12 = f32[888,256]{1,0:T(8,128)} copy(f32[888,256]{1,0:T(8,128)S(1)} %shard_map.100) | data formatting | bytes 1818624

commit v4 on v3

--- a/solution.py
+++ b/solution.py
@@ -1,4 +1,5 @@
 import functools
+import itertools
 
 import jax
 import jax.numpy as jnp
@@ -53,7 +54,6 @@
     sizes,
     mult_h,
     comp_h,
-    expd_h,
     octs_h,
     fars_h,
     l7_h,
@@ -61,10 +61,9 @@
     l5_h,
     l4_h,
     l3_h,
-    outv,
+    local_ref,
     mult,
     comp,
-    expd,
     octs,
     fars,
     l7,
@@ -116,7 +115,6 @@
                 (l4_h, l4),
                 (l3_h, l3),
                 (fars_h, fars),
-                (expd_h, expd),
             ]
         )
     ]
@@ -144,7 +142,6 @@
     loads[0].wait()
     loads[1].wait()
     loads[8].start()
-    loads[9].start()
     seven = tn(mult[...], comp[...]).astype(BF16)
     own[...] = seven
     put_rows(c7f, 0, b7, seven.astype(F32))
@@ -193,7 +190,7 @@
         halo_copy(small.at[pl.ds(block, block), :], small, block, 2, left, 3),
     ]
 
-    def spread(k, carry):
+    def spread(k):
         pltpu.make_async_remote_copy(
             src_ref=every.at[mine, :],
             dst_ref=every.at[mine, :],
@@ -202,11 +199,11 @@
             device_id=place(lax.rem(me + k, n)),
             device_id_type=MESH,
         ).start()
-        return carry
-
-    lax.fori_loop(1, n, spread, 0)
+
     for copy in small_sends:
         copy.start()
+    peers = iter(range(1, n))
+    each = -(-2 * (n - 1) // classes)
 
     for k in range(3, 8):
         loads[k].wait()
@@ -232,9 +229,15 @@
     p3 = jnp.where(p3 >= 0, p3 + base3, -1)
     row = iota((16, 1), 0)
 
+    def pick_own(c):
+        own_pick[c] = nn(onehot(p7[:, c : c + 1], b7, b7), own[...]).astype(BF16)
+
     for c in range(classes):
+        for k in itertools.islice(peers, each):
+            spread(k)
         col = p7[:, c : c + 1]
-        own_pick[c] = nn(onehot(col, b7, b7), own[...]).astype(BF16)
+        if c < classes // 2:
+            pick_own(c)
         hot[c, :, 0:b7] = onehot(col, b7, 0)
         hot[c, :, b7 : 2 * b7] = onehot(col, b7, 2 * b7)
         tail = jnp.where(row == b5, p4[c : c + 1, :], p5[:, c : c + 1])
@@ -245,7 +248,7 @@
     loads[8].wait()
     rest = every.at[pl.ds(0, (n - 1) * 8), :]
     pltpu.make_async_copy(rest, rest, all_recv).wait()
-    for copy in halo_sends + small_sends:
+    for copy in small_sends:
         copy.wait_recv()
 
     def coarser():
@@ -297,7 +300,11 @@
                 yield
 
     chain = coarser()
-    next(chain, None)
+    for c in range(classes // 2, classes):
+        next(chain, None)
+        pick_own(c)
+    for copy in halo_sends:
+        copy.wait_recv()
     for c in range(classes):
         next(chain, None)
         picked = nn(hot[c], halo[...]) + own_pick[c].astype(F32)
@@ -307,14 +314,8 @@
             acc[...] += nt(picked.astype(BF16), fars[c])
     for _ in chain:
         pass
-    local7 = (acc[...] + take_rows(d7, 0, b7)).astype(BF16)
-
-    loads[9].wait()
-    surface = expd.shape[0]
-    step = 304
-    for start in range(0, surface, step):
-        stop = min(start + step, surface)
-        outv[start:stop, :] = nt(expd[start:stop, :], local7)
+    local_ref[...] = (acc[...] + take_rows(d7, 0, b7)).astype(BF16)
+
     for copy in halo_sends + small_sends:
         copy.wait_send()
     pltpu.make_async_copy(rest, rest, all_send).wait()
@@ -322,7 +323,7 @@
 
 def on_device(axes, counts, *args):
     mult, comp, expd, octs, fars, l7, l6, l5, l4, l3 = args
-    args = (mult, comp.T, expd, octs, fars, l7, l6, l5.T, l4, l3.T)
+    args = (mult, comp.T, octs, fars, l7, l6, l5.T, l4, l3.T)
     n = counts[0] * counts[1]
     b7, b6, b5 = l7.shape[1], l6.shape[1], l5.shape[1]
     nb4, nb3 = l4.shape[1], l3.shape[1]
@@ -347,15 +348,15 @@
         pltpu.VMEM((b7, r), F32),
         pltpu.VMEM((r // 128, 64, 128), F32),
         pltpu.VMEM((r // 128, b7, 128), F32),
-        pltpu.SemaphoreType.DMA((10,)),
+        pltpu.SemaphoreType.DMA((9,)),
         pltpu.SemaphoreType.DMA((4,)),
         pltpu.SemaphoreType.DMA((4,)),
         pltpu.SemaphoreType.DMA,
         pltpu.SemaphoreType.DMA,
     ]
-    return pl.pallas_call(
+    local = pl.pallas_call(
         functools.partial(kernel, (axes, counts, classes, nb4, nb3)),
-        out_shape=pltpu.VMEM((expd.shape[0], b7), F32),
+        out_shape=pltpu.VMEM((b7, r), BF16),
         in_specs=[pl.BlockSpec(memory_space=pltpu.HBM)] * len(args),
         out_specs=pl.BlockSpec(memory_space=pltpu.VMEM),
         scratch_shapes=scratch,
@@ -363,6 +364,7 @@
             collective_id=0, has_side_effects=True, vmem_limit_bytes=50 * 1024 * 1024
         ),
     )(*[pltpu.with_memory_space_constraint(a, pltpu.HBM) for a in args])
+    return nt(expd, local)
 
 
 def solution(mesh):

time: 20.7 us -> 20.9 us (level)
  matrix products: 0 us -> 1.24 us
  local copies, waits for them, and re-layouts: 0.92 us -> 0.01 us
    dot_general x0 -> x1, matrix products: none -> 1.24 us  [nt(): lax.dot_general(a, b, (((1,), (1,)), ((), ())), preferred_element_type=F32)]
    unnamed x1 -> x2, local copies, waits for them, and re-layouts: 0.92 us -> 0.01 us
where the time goes in v4:
time: 20.9 us; the launch traced here: 20.7 us
  Pallas kernels  19.5 us (93%)
  matrix products  1.24 us (6%)
    pallas_call x1, Pallas kernels, on_device(): pl.pallas_call(functools.partial(kernel, (axes, counts, classes, nb4, nb3...  19.5 us
    dot_general x1, matrix products, nt(): lax.dot_general(a, b, (((1,), (1,)), ((), ())), preferred_element_type=F32)  1.24 us

profile of v4, /device:TPU:0, one launch (start us, length us, event | category | flops | bytes accessed | tf_op | source)
XLA Modules:
  0.0 20.7 jit_solution(1342447126889548063)
XLA Ops:
  0.0 0.0 copy-start
  0.0 19.5 %shard_map.100 = bf16[256,256]{1,0:T(8,128)(2,1)S(1)} custom-call(bf16[888,256]{1,0:T(8,128)(2,1)} %mult_h.1, bf16[888,256]{1,0:T(8,128)(2,1)} %bitcast.7, bf16[8,256,256]{2,1,0:T(8,128)(2,1)} %octs_h.1, bf16[16,256,256]{2,1,0:T(8,128)(2,1)} %fars_h.1, s32[16,256]{1,0:T(8,128)} %l7_h.1, s32[16,32]{1,0:T(8,128)} %l6_h.1, s32[4,16]{1,0:T(4,128)} %bitcast.8, ...), custom_call_target="tpu_custom_call" | custom-call | tf_op jit(solution)/shard_map/pallas_call | solution.py:357
  19.5 0.0 copy-done
  19.5 1.2 %convolution_bitcast_fusion = f32[888,256]{1,0:T(8,128)} fusion(bf16[256,256]{1,0:T(8,128)(2,1)S(1)} %shard_map.100, bf16[888,256]{1,0:T(8,128)(2,1)S(1)} %copy-done), kind=kOutput, calls=%fused_computation | convolution fusion | flops 116391936 | bytes 1495040 | tf_op jit(solution)/shard_map/dot_general | solution.py:17
Async XLA Ops:
  0.0 19.5 %copy-start = (bf16[888,256]{1,0:T(8,128)(2,1)S(1)}, bf16[888,256]{1,0:T(8,128)(2,1)}, u32[]{:S(2)}) copy-start(bf16[888,256]{1,0:T(8,128)(2,1)} %param.12) | copy-start | bytes 1363972

commit v5 on v4

--- a/solution.py
+++ b/solution.py
@@ -27,6 +27,14 @@
 
 def iota(shape, axis):
     return lax.broadcasted_iota(jnp.int32, shape, axis)
+
+
+def beside(parts):
+    return jnp.concatenate(list(parts), axis=1)
+
+
+def lanes_of(ops):
+    return beside(ops[k] for k in range(ops.shape[0]))
 
 
 def take_rows(ref, start, rows, stride=1):
@@ -79,6 +87,7 @@
     small,
     every,
     own_pick,
+    hot_own,
     hot,
     hot_small,
     acc,
@@ -168,15 +177,10 @@
         copy.start()
 
     loads[2].wait()
-    total = jnp.zeros((b6, octs.shape[1]), F32)
-    for o in range(8):
-        total = total + nt(take_rows(c7f, o, b6, 8).astype(BF16), octs[o])
-    six = total.astype(BF16)
+    up = lanes_of(octs)
+    six = nt(beside(take_rows(c7f, o, b6, 8).astype(BF16) for o in range(8)), up).astype(BF16)
     put_rows(c6f, 0, b6, six.astype(F32))
-    total = jnp.zeros((16, octs.shape[1]), F32)
-    for o in range(8):
-        total = total + nt(take_rows(c6f, o, 16, 8).astype(BF16), octs[o])
-    five = total.astype(BF16)
+    five = nt(beside(take_rows(c6f, o, 16, 8).astype(BF16) for o in range(8)), up).astype(BF16)
     small[block : block + b6, :] = six
     small[block + b6 : 2 * block, :] = five
     fivef = five.astype(F32)
@@ -203,7 +207,7 @@
     for copy in small_sends:
         copy.start()
     peers = iter(range(1, n))
-    each = -(-2 * (n - 1) // classes)
+    each = -(-4 * (n - 1) // classes)
 
     for k in range(3, 8):
         loads[k].wait()
@@ -229,52 +233,48 @@
     p3 = jnp.where(p3 >= 0, p3 + base3, -1)
     row = iota((16, 1), 0)
 
-    def pick_own(c):
-        own_pick[c] = nn(onehot(p7[:, c : c + 1], b7, b7), own[...]).astype(BF16)
+    group = 4
 
     for c in range(classes):
         for k in itertools.islice(peers, each):
             spread(k)
         col = p7[:, c : c + 1]
-        if c < classes // 2:
-            pick_own(c)
-        hot[c, :, 0:b7] = onehot(col, b7, 0)
-        hot[c, :, b7 : 2 * b7] = onehot(col, b7, 2 * b7)
+        rows = pl.ds(c * b7, b7)
+        hot_own[rows, :] = onehot(col, b7, b7)
+        hot[rows, 0:b7] = onehot(col, b7, 0)
+        hot[rows, b7 : 2 * b7] = onehot(col, b7, 2 * b7)
         tail = jnp.where(row == b5, p4[c : c + 1, :], p5[:, c : c + 1])
         tail = jnp.where(row == b5 + 1, p3[c : c + 1, :], tail)
         cols = jnp.concatenate([column(p6[c : c + 1, :], b6).astype(jnp.int32), tail], axis=0)
-        hot_small[c] = onehot(cols, depth)
+        hot_small[c * block : (c + 1) * block, :] = onehot(cols, depth)
+        if c % group == group - 1:
+            rows = pl.ds((c + 1 - group) * b7, group * b7)
+            own_pick[rows, :] = nn(hot_own[rows, :], own[...]).astype(BF16)
 
     loads[8].wait()
     rest = every.at[pl.ds(0, (n - 1) * 8), :]
     pltpu.make_async_copy(rest, rest, all_recv).wait()
-    for copy in small_sends:
+    for copy in halo_sends + small_sends:
         copy.wait_recv()
 
     def coarser():
-        total = jnp.zeros((nb4, octs.shape[1]), F32)
+        parts = []
         for o in range(8):
             at = (o // b5) * 8 + o % b5
             low = every[pl.ds(at, nb4, stride=8 * per4), :]
             high = every[pl.ds(at + b5, nb4, stride=8 * per4), :]
-            total = total + nt(jnp.concatenate([low, high], axis=1).astype(BF16), octs[o])
-            if o % 4 == 3:
-                yield
-        four = total.astype(BF16)
+            parts += [low.astype(BF16), high.astype(BF16)]
+        four = nt(beside(parts), up).astype(BF16)
         put_rows(c4f, 0, nb4, four.astype(F32))
         small[base4 : base4 + nb4, :] = four
-        total = jnp.zeros((rows3, octs.shape[1]), F32)
-        for o in range(8):
-            total = total + nt(take_rows(c4f, o, rows3, 8).astype(BF16), octs[o])
-            if o % 4 == 3:
-                yield
-        small[base3 : base3 + rows3, :] = total.astype(BF16)
-        far = jnp.zeros((block, octs.shape[1]), F32)
-        for c in range(classes):
-            lesser = nn(hot_small[c], small[...]).astype(BF16)
-            far = far + nt(lesser, fars[c])
-            if c % 4 == 3:
-                yield
+        yield
+        parts = [take_rows(c4f, o, rows3, 8).astype(BF16) for o in range(8)]
+        small[base3 : base3 + rows3, :] = nt(beside(parts), up).astype(BF16)
+        yield
+        lesser = nn(hot_small[...], small[...]).astype(BF16)
+        lesser = beside(lesser[c * block : (c + 1) * block, :] for c in range(classes))
+        far = nt(lesser, lanes_of(fars))
+        yield
         far6, far5 = 2.0 * far[0:b6, :], 4.0 * far[b6:block, :]
         far4 = 8.0 * far[b6 + b5 : b6 + b5 + 1, :]
         far3 = 16.0 * far[b6 + b5 + 1 : b6 + b5 + 2, :]
@@ -282,12 +282,10 @@
         down = nn(jnp.broadcast_to(far3, wide).astype(BF16), octs[t4 % 8])
         local4 = jnp.broadcast_to(far4 + down[0:1, :], wide)
         yield
-        local5 = far5
         first = (me % per4) * b5
-        for k in range(b5):
-            local5 = local5 + nn(
-                jnp.where(iota(wide, 0) == k, local4, 0.0).astype(BF16), octs[first + k]
-            )
+        parts = [jnp.where(iota(wide, 0) == k, local4, 0.0).astype(BF16) for k in range(b5)]
+        ops = octs[pl.ds(first, b5)].reshape(b5 * wide[1], wide[1])
+        local5 = far5 + nn(beside(parts), ops)
         local5 = local5.astype(BF16)
         yield
         for o in range(8):
@@ -300,18 +298,14 @@
                 yield
 
     chain = coarser()
-    for c in range(classes // 2, classes):
+    for start in range(0, classes, group):
         next(chain, None)
-        pick_own(c)
-    for copy in halo_sends:
-        copy.wait_recv()
-    for c in range(classes):
+        rows = pl.ds(start * b7, group * b7)
+        picked = (nn(hot[rows, :], halo[...]) + own_pick[rows, :].astype(F32)).astype(BF16)
         next(chain, None)
-        picked = nn(hot[c], halo[...]) + own_pick[c].astype(F32)
-        if c == 0:
-            acc[...] = nt(picked.astype(BF16), fars[c])
-        else:
-            acc[...] += nt(picked.astype(BF16), fars[c])
+        wide_picked = beside(picked[k * b7 : (k + 1) * b7, :] for k in range(group))
+        far = nt(wide_picked, lanes_of(fars.at[pl.ds(start, group)]))
+        acc[...] = far if start == 0 else acc[...] + far
     for _ in chain:
         pass
     local_ref[...] = (acc[...] + take_rows(d7, 0, b7)).astype(BF16)
@@ -342,9 +336,10 @@
         pltpu.VMEM((2 * b7, r), BF16),
         pltpu.VMEM((depth, r), BF16),
         pltpu.VMEM((n * 8, r // 2), F32),
-        pltpu.VMEM((classes, b7, r), BF16),
-        pltpu.VMEM((classes, b7, 2 * b7), BF16),
-        pltpu.VMEM((classes, block, depth), BF16),
+        pltpu.VMEM((classes * b7, r), BF16),
+        pltpu.VMEM((classes * b7, b7), BF16),
+        pltpu.VMEM((classes * b7, 2 * b7), BF16),
+        pltpu.VMEM((classes * block, depth), BF16),
         pltpu.VMEM((b7, r), F32),
         pltpu.VMEM((r // 128, 64, 128), F32),
         pltpu.VMEM((r // 128, b7, 128), F32),

time: 20.9 us -> 19.9 us (0.952)
  Pallas kernels: 19.5 us -> 18.5 us
    pallas_call x1, Pallas kernels: 19.5 us -> 18.5 us  [on_device(): pl.pallas_call(functools.partial(kernel, (axes, counts, classes, nb4, nb3...]
where the time goes in v5:
time: 19.9 us; the launch traced here: 19.8 us
  Pallas kernels  18.5 us (93%)
  matrix products  1.24 us (6%)
    pallas_call x1, Pallas kernels, on_device(): pl.pallas_call(functools.partial(kernel, (axes, counts, classes, nb4, nb3...  18.5 us
    dot_general x1, matrix products, nt(): lax.dot_general(a, b, (((1,), (1,)), ((), ())), preferred_element_type=F32)  1.24 us

profile of v5, /device:TPU:0, one launch (start us, length us, event | category | flops | bytes accessed | tf_op | source)
XLA Modules:
  0.0 19.8 jit_solution(18012656710567506394)
XLA Ops:
  0.0 0.0 copy-start
  0.0 18.5 %shard_map.100 = bf16[256,256]{1,0:T(8,128)(2,1)S(1)} custom-call(bf16[888,256]{1,0:T(8,128)(2,1)} %mult_h.1, bf16[888,256]{1,0:T(8,128)(2,1)} %bitcast.7, bf16[8,256,256]{2,1,0:T(8,128)(2,1)} %octs_h.1, bf16[16,256,256]{2,1,0:T(8,128)(2,1)} %fars_h.1, s32[16,256]{1,0:T(8,128)} %l7_h.1, s32[16,32]{1,0:T(8,128)} %l6_h.1, s32[4,16]{1,0:T(4,128)} %bitcast.8, ...), custom_call_target="tpu_custom_call" | custom-call | tf_op jit(solution)/shard_map/pallas_call | solution.py:352
  18.5 0.0 copy-done
  18.5 1.2 %convolution_bitcast_fusion = f32[888,256]{1,0:T(8,128)} fusion(bf16[256,256]{1,0:T(8,128)(2,1)S(1)} %shard_map.100, bf16[888,256]{1,0:T(8,128)(2,1)S(1)} %copy-done), kind=kOutput, calls=%fused_computation | convolution fusion | flops 116391936 | bytes 1495040 | tf_op jit(solution)/shard_map/dot_general | solution.py:17
Async XLA Ops:
  0.0 18.5 %copy-start = (bf16[888,256]{1,0:T(8,128)(2,1)S(1)}, bf16[888,256]{1,0:T(8,128)(2,1)}, u32[]{:S(2)}) copy-start(bf16[888,256]{1,0:T(8,128)(2,1)} %param.12) | copy-start | bytes 1363972

commit v6 on v5

--- a/solution.py
+++ b/solution.py
@@ -234,15 +234,17 @@
     row = iota((16, 1), 0)
 
     group = 4
+    lane7 = iota((b7, b7), 1).astype(jnp.int16)
+    one, zero = jnp.ones((b7, b7), BF16), jnp.zeros((b7, b7), BF16)
 
     for c in range(classes):
         for k in itertools.islice(peers, each):
             spread(k)
-        col = p7[:, c : c + 1]
+        col = jnp.broadcast_to(p7[:, c : c + 1], (b7, b7)).astype(jnp.int16)
         rows = pl.ds(c * b7, b7)
-        hot_own[rows, :] = onehot(col, b7, b7)
-        hot[rows, 0:b7] = onehot(col, b7, 0)
-        hot[rows, b7 : 2 * b7] = onehot(col, b7, 2 * b7)
+        hot_own[rows, :] = jnp.where(col == lane7 + b7, one, zero)
+        hot[rows, 0:b7] = jnp.where(col == lane7, one, zero)
+        hot[rows, b7 : 2 * b7] = jnp.where(col == lane7 + 2 * b7, one, zero)
         tail = jnp.where(row == b5, p4[c : c + 1, :], p5[:, c : c + 1])
         tail = jnp.where(row == b5 + 1, p3[c : c + 1, :], tail)
         cols = jnp.concatenate([column(p6[c : c + 1, :], b6).astype(jnp.int32), tail], axis=0)
@@ -252,9 +254,7 @@
             own_pick[rows, :] = nn(hot_own[rows, :], own[...]).astype(BF16)
 
     loads[8].wait()
-    rest = every.at[pl.ds(0, (n - 1) * 8), :]
-    pltpu.make_async_copy(rest, rest, all_recv).wait()
-    for copy in halo_sends + small_sends:
+    for copy in halo_sends:
         copy.wait_recv()
 
     def coarser():
@@ -297,12 +297,19 @@
             if o % 4 == 3:
                 yield
 
+    rest = every.at[pl.ds(0, (n - 1) * 8), :]
     chain = coarser()
     for start in range(0, classes, group):
-        next(chain, None)
+        if start == group:
+            pltpu.make_async_copy(rest, rest, all_recv).wait()
+            for copy in small_sends:
+                copy.wait_recv()
+        if start >= group:
+            next(chain, None)
         rows = pl.ds(start * b7, group * b7)
         picked = (nn(hot[rows, :], halo[...]) + own_pick[rows, :].astype(F32)).astype(BF16)
-        next(chain, None)
+        if start >= group:
+            next(chain, None)
         wide_picked = beside(picked[k * b7 : (k + 1) * b7, :] for k in range(group))
         far = nt(wide_picked, lanes_of(fars.at[pl.ds(start, group)]))
         acc[...] = far if start == 0 else acc[...] + far

time: 19.9 us -> 19.2 us (0.965)
  Pallas kernels: 18.5 us -> 17.8 us
    pallas_call x1, Pallas kernels: 18.5 us -> 17.8 us  [on_device(): pl.pallas_call(functools.partial(kernel, (axes, counts, classes, nb4, nb3...]
where the time goes in v6:
time: 19.2 us; the launch traced here: 19 us
  Pallas kernels  17.8 us (93%)
  matrix products  1.23 us (6%)
    pallas_call x1, Pallas kernels, on_device(): pl.pallas_call(functools.partial(kernel, (axes, counts, classes, nb4, nb3...  17.8 us
    dot_general x1, matrix products, nt(): lax.dot_general(a, b, (((1,), (1,)), ((), ())), preferred_element_type=F32)  1.23 us

profile of v6, /device:TPU:0, one launch (start us, length us, event | category | flops | bytes accessed | tf_op | source)
XLA Modules:
  0.0 19.0 jit_solution(11613905187407712918)
XLA Ops:
  0.0 0.0 copy-start
  0.0 17.8 %shard_map.100 = bf16[256,256]{1,0:T(8,128)(2,1)S(1)} custom-call(bf16[888,256]{1,0:T(8,128)(2,1)} %mult_h.1, bf16[888,256]{1,0:T(8,128)(2,1)} %bitcast.7, bf16[8,256,256]{2,1,0:T(8,128)(2,1)} %octs_h.1, bf16[16,256,256]{2,1,0:T(8,128)(2,1)} %fars_h.1, s32[16,256]{1,0:T(8,128)} %l7_h.1, s32[16,32]{1,0:T(8,128)} %l6_h.1, s32[4,16]{1,0:T(4,128)} %bitcast.8, ...), custom_call_target="tpu_custom_call" | custom-call | tf_op jit(solution)/shard_map/pallas_call | solution.py:359
  17.8 0.0 copy-done
  17.8 1.2 %convolution_bitcast_fusion = f32[888,256]{1,0:T(8,128)} fusion(bf16[256,256]{1,0:T(8,128)(2,1)S(1)} %shard_map.100, bf16[888,256]{1,0:T(8,128)(2,1)S(1)} %copy-done), kind=kOutput, calls=%fused_computation | convolution fusion | flops 116391936 | bytes 1495040 | tf_op jit(solution)/shard_map/dot_general | solution.py:17
Async XLA Ops:
  0.0 17.8 %copy-start = (bf16[888,256]{1,0:T(8,128)(2,1)S(1)}, bf16[888,256]{1,0:T(8,128)(2,1)}, u32[]{:S(2)}) copy-start(bf16[888,256]{1,0:T(8,128)(2,1)} %param.12) | copy-start | bytes 1363972

commit v7 on v6

--- a/solution.py
+++ b/solution.py
@@ -117,12 +117,12 @@
             [
                 (comp_h, comp),
                 (mult_h, mult),
-                (octs_h, octs),
                 (l7_h, l7),
                 (l6_h, l6),
                 (l5_h, l5),
                 (l4_h, l4),
                 (l3_h, l3),
+                (octs_h, octs),
                 (fars_h, fars),
             ]
         )
@@ -148,68 +148,7 @@
     t4 = me // per4
     t3 = t4 // 8
 
-    loads[0].wait()
-    loads[1].wait()
-    loads[8].start()
-    seven = tn(mult[...], comp[...]).astype(BF16)
-    own[...] = seven
-    put_rows(c7f, 0, b7, seven.astype(F32))
-
-    pl.semaphore_wait(barrier, n - 1)
-    right = place(lax.rem(me + 1, n))
-    left = place(lax.rem(me + n - 1, n))
-
-    def halo_copy(src, ref, rows, slot, peer, index):
-        return pltpu.make_async_remote_copy(
-            src_ref=src,
-            dst_ref=ref.at[pl.ds(slot * rows, rows), :],
-            send_sem=send_sem.at[index],
-            recv_sem=recv_sem.at[index],
-            device_id=peer,
-            device_id_type=MESH,
-        )
-
-    halo_sends = [
-        halo_copy(own, halo, b7, 0, right, 0),
-        halo_copy(own, halo, b7, 1, left, 1),
-    ]
-    for copy in halo_sends:
-        copy.start()
-
-    loads[2].wait()
-    up = lanes_of(octs)
-    six = nt(beside(take_rows(c7f, o, b6, 8).astype(BF16) for o in range(8)), up).astype(BF16)
-    put_rows(c6f, 0, b6, six.astype(F32))
-    five = nt(beside(take_rows(c6f, o, 16, 8).astype(BF16) for o in range(8)), up).astype(BF16)
-    small[block : block + b6, :] = six
-    small[block + b6 : 2 * block, :] = five
-    fivef = five.astype(F32)
-    half = octs.shape[1] // 2
-    tile = jnp.concatenate([fivef[0:b5, :half], fivef[0:b5, half:]], axis=0)
-    mine = pl.ds(pl.multiple_of(me * 8, 8), 8)
-    every[mine, :] = tile
-
-    small_sends = [
-        halo_copy(small.at[pl.ds(block, block), :], small, block, 0, right, 2),
-        halo_copy(small.at[pl.ds(block, block), :], small, block, 2, left, 3),
-    ]
-
-    def spread(k):
-        pltpu.make_async_remote_copy(
-            src_ref=every.at[mine, :],
-            dst_ref=every.at[mine, :],
-            send_sem=all_send,
-            recv_sem=all_recv,
-            device_id=place(lax.rem(me + k, n)),
-            device_id_type=MESH,
-        ).start()
-
-    for copy in small_sends:
-        copy.start()
-    peers = iter(range(1, n))
-    each = -(-4 * (n - 1) // classes)
-
-    for k in range(3, 8):
+    for k in range(2, 7):
         loads[k].wait()
     e7 = l7[...]
     p7 = jnp.where(e7 >= 0, e7 - (me * b7 - b7), -1).astype(F32).T.astype(jnp.int32)
@@ -237,9 +176,7 @@
     lane7 = iota((b7, b7), 1).astype(jnp.int16)
     one, zero = jnp.ones((b7, b7), BF16), jnp.zeros((b7, b7), BF16)
 
-    for c in range(classes):
-        for k in itertools.islice(peers, each):
-            spread(k)
+    def build(c):
         col = jnp.broadcast_to(p7[:, c : c + 1], (b7, b7)).astype(jnp.int16)
         rows = pl.ds(c * b7, b7)
         hot_own[rows, :] = jnp.where(col == lane7 + b7, one, zero)
@@ -249,6 +186,76 @@
         tail = jnp.where(row == b5 + 1, p3[c : c + 1, :], tail)
         cols = jnp.concatenate([column(p6[c : c + 1, :], b6).astype(jnp.int32), tail], axis=0)
         hot_small[c * block : (c + 1) * block, :] = onehot(cols, depth)
+
+    for c in range(group):
+        build(c)
+
+    loads[0].wait()
+    loads[1].wait()
+    loads[8].start()
+    seven = tn(mult[...], comp[...]).astype(BF16)
+    own[...] = seven
+    put_rows(c7f, 0, b7, seven.astype(F32))
+
+    pl.semaphore_wait(barrier, n - 1)
+    right = place(lax.rem(me + 1, n))
+    left = place(lax.rem(me + n - 1, n))
+
+    def halo_copy(src, ref, rows, slot, peer, index):
+        return pltpu.make_async_remote_copy(
+            src_ref=src,
+            dst_ref=ref.at[pl.ds(slot * rows, rows), :],
+            send_sem=send_sem.at[index],
+            recv_sem=recv_sem.at[index],
+            device_id=peer,
+            device_id_type=MESH,
+        )
+
+    halo_sends = [
+        halo_copy(own, halo, b7, 0, right, 0),
+        halo_copy(own, halo, b7, 1, left, 1),
+    ]
+    for copy in halo_sends:
+        copy.start()
+
+    loads[7].wait()
+    up = lanes_of(octs)
+    six = nt(beside(take_rows(c7f, o, b6, 8).astype(BF16) for o in range(8)), up).astype(BF16)
+    put_rows(c6f, 0, b6, six.astype(F32))
+    five = nt(beside(take_rows(c6f, o, 16, 8).astype(BF16) for o in range(8)), up).astype(BF16)
+    small[block : block + b6, :] = six
+    small[block + b6 : 2 * block, :] = five
+    fivef = five.astype(F32)
+    half = octs.shape[1] // 2
+    tile = jnp.concatenate([fivef[0:b5, :half], fivef[0:b5, half:]], axis=0)
+    mine = pl.ds(pl.multiple_of(me * 8, 8), 8)
+    every[mine, :] = tile
+
+    small_sends = [
+        halo_copy(small.at[pl.ds(block, block), :], small, block, 0, right, 2),
+        halo_copy(small.at[pl.ds(block, block), :], small, block, 2, left, 3),
+    ]
+
+    def spread(k):
+        pltpu.make_async_remote_copy(
+            src_ref=every.at[mine, :],
+            dst_ref=every.at[mine, :],
+            send_sem=all_send,
+            recv_sem=all_recv,
+            device_id=place(lax.rem(me + k, n)),
+            device_id_type=MESH,
+        ).start()
+
+    for copy in small_sends:
+        copy.start()
+    peers = iter(range(1, n))
+    each = -(-4 * (n - 1) // classes)
+
+    for c in range(classes):
+        for k in itertools.islice(peers, each):
+            spread(k)
+        if c >= group:
+            build(c)
         if c % group == group - 1:
             rows = pl.ds((c + 1 - group) * b7, group * b7)
             own_pick[rows, :] = nn(hot_own[rows, :], own[...]).astype(BF16)

time: 19.2 us -> 19.2 us (level)
  no operation moved by 1% of the time
where the time goes in v7:
time: 19.2 us; the launch traced here: 19 us
  Pallas kernels  17.8 us (93%)
  matrix products  1.23 us (6%)
    pallas_call x1, Pallas kernels, on_device(): pl.pallas_call(functools.partial(kernel, (axes, counts, classes, nb4, nb3...  17.8 us
    dot_general x1, matrix products, nt(): lax.dot_general(a, b, (((1,), (1,)), ((), ())), preferred_element_type=F32)  1.23 us

profile of v7, /device:TPU:0, one launch (start us, length us, event | category | flops | bytes accessed | tf_op | source)
XLA Modules:
  0.0 19.0 jit_solution(3335476316197156970)
XLA Ops:
  0.0 0.0 copy-start
  0.0 17.8 %shard_map.100 = bf16[256,256]{1,0:T(8,128)(2,1)S(1)} custom-call(bf16[888,256]{1,0:T(8,128)(2,1)} %mult_h.1, bf16[888,256]{1,0:T(8,128)(2,1)} %bitcast.7, bf16[8,256,256]{2,1,0:T(8,128)(2,1)} %octs_h.1, bf16[16,256,256]{2,1,0:T(8,128)(2,1)} %fars_h.1, s32[16,256]{1,0:T(8,128)} %l7_h.1, s32[16,32]{1,0:T(8,128)} %l6_h.1, s32[4,16]{1,0:T(4,128)} %bitcast.8, ...), custom_call_target="tpu_custom_call" | custom-call | tf_op jit(solution)/shard_map/pallas_call | solution.py:366
  17.8 0.0 copy-done
  17.8 1.2 %convolution_bitcast_fusion = f32[888,256]{1,0:T(8,128)} fusion(bf16[256,256]{1,0:T(8,128)(2,1)S(1)} %shard_map.100, bf16[888,256]{1,0:T(8,128)(2,1)S(1)} %copy-done), kind=kOutput, calls=%fused_computation | convolution fusion | flops 116391936 | bytes 1495040 | tf_op jit(solution)/shard_map/dot_general | solution.py:17
Async XLA Ops:
  0.0 17.8 %copy-start = (bf16[888,256]{1,0:T(8,128)(2,1)S(1)}, bf16[888,256]{1,0:T(8,128)(2,1)}, u32[]{:S(2)}) copy-start(bf16[888,256]{1,0:T(8,128)(2,1)} %param.12) | copy-start | bytes 1363972

commit v8 on v7

--- a/solution.py
+++ b/solution.py
@@ -249,7 +249,7 @@
     for copy in small_sends:
         copy.start()
     peers = iter(range(1, n))
-    each = -(-4 * (n - 1) // classes)
+    each = n - 1
 
     for c in range(classes):
         for k in itertools.islice(peers, each):

time: 19.2 us -> 19.2 us (level)
  no operation moved by 1% of the time
where the time goes in v8:
time: 19.2 us; the launch traced here: 19 us
  Pallas kernels  17.8 us (93%)
  matrix products  1.23 us (6%)
    pallas_call x1, Pallas kernels, on_device(): pl.pallas_call(functools.partial(kernel, (axes, counts, classes, nb4, nb3...  17.8 us
    dot_general x1, matrix products, nt(): lax.dot_general(a, b, (((1,), (1,)), ((), ())), preferred_element_type=F32)  1.23 us

profile of v8, /device:TPU:0, one launch (start us, length us, event | category | flops | bytes accessed | tf_op | source)
XLA Modules:
  0.0 19.0 jit_solution(3335476316197156970)
XLA Ops:
  0.0 0.0 copy-start
  0.0 17.8 %shard_map.100 = bf16[256,256]{1,0:T(8,128)(2,1)S(1)} custom-call(bf16[888,256]{1,0:T(8,128)(2,1)} %mult_h.1, bf16[888,256]{1,0:T(8,128)(2,1)} %bitcast.7, bf16[8,256,256]{2,1,0:T(8,128)(2,1)} %octs_h.1, bf16[16,256,256]{2,1,0:T(8,128)(2,1)} %fars_h.1, s32[16,256]{1,0:T(8,128)} %l7_h.1, s32[16,32]{1,0:T(8,128)} %l6_h.1, s32[4,16]{1,0:T(4,128)} %bitcast.8, ...), custom_call_target="tpu_custom_call" | custom-call | tf_op jit(solution)/shard_map/pallas_call | solution.py:366
  17.8 0.0 copy-done
  17.8 1.2 %convolution_bitcast_fusion = f32[888,256]{1,0:T(8,128)} fusion(bf16[256,256]{1,0:T(8,128)(2,1)S(1)} %shard_map.100, bf16[888,256]{1,0:T(8,128)(2,1)S(1)} %copy-done), kind=kOutput, calls=%fused_computation | convolution fusion | flops 116391936 | bytes 1495040 | tf_op jit(solution)/shard_map/dot_general | solution.py:17
Async XLA Ops:
  0.0 17.8 %copy-start = (bf16[888,256]{1,0:T(8,128)(2,1)S(1)}, bf16[888,256]{1,0:T(8,128)(2,1)}, u32[]{:S(2)}) copy-start(bf16[888,256]{1,0:T(8,128)(2,1)} %param.12) | copy-start | bytes 1363972
